TPU v7x, 32 devices: a whole 2x2x4 slice. The times are simulated.
32 devices in a mesh: dp: 2 (over x), row: 4 (over y, core), col: 4 (over z).
Axes of the slice: x: 2, y: 2, z: 4, core: 2. Of those that a mesh axis runs over, the one named last changes fastest.
Arguments:
- tokens: bfloat16 [8192, 1024], P(('dp', 'col'), 'row'), may hold values from -8 to 8
- w_qkv: bfloat16 [3, 1024, 1024], P(None, 'row', 'col'), may hold values from -0.1875 to 0.1875
- bias_qv: bfloat16 [2, 1024], P(None, 'col'), may hold values from -3 to 3
- w_out: bfloat16 [1024, 1024], P('col', 'row'), may hold values from -2 to 2
- bias_out: bfloat16 [1024], P('row'), may hold values from -3 to 3
- gain_one: bfloat16 [1024], P('row'), may hold values from 0.25 to 1.75
- shift_one: bfloat16 [1024], P('row'), may hold values from -3 to 3
- w_in: bfloat16 [1024, 4096], P('row', 'col'), may hold values from -0.1875 to 0.1875
- bias_in: bfloat16 [4096], P('col'), may hold values from -3 to 3
- w_back: bfloat16 [4096, 1024], P('col', 'row'), may hold values from -0.09375 to 0.09375
- bias_back: bfloat16 [1024], P('row'), may hold values from -3 to 3
- gain_two: bfloat16 [1024], P('row'), may hold values from 0.25 to 1.75
- shift_two: bfloat16 [1024], P('row'), may hold values from -3 to 3
- cotangent: bfloat16 [8192, 1024], P(('dp', 'col'), 'row'), may hold values from -8 to 8
Outputs:
- output: bfloat16 [8192, 1024], P(('dp', 'col'), 'row')
- grad_tokens: float32 [8192, 1024], P(('dp', 'col'), 'row')
- grad_w_qkv: float32 [3, 1024, 1024], P(None, 'row', 'col')
- grad_bias_qv: float32 [2, 1024], P(None, 'col')
- grad_w_out: float32 [1024, 1024], P('col', 'row')
- grad_bias_out: float32 [1024], P('row')
- grad_gain_one: float32 [1024], P('row')
- grad_shift_one: float32 [1024], P('row')
- grad_w_in: float32 [1024, 4096], P('row', 'col')
- grad_bias_in: float32 [4096], P('col')
- grad_w_back: float32 [4096, 1024], P('col', 'row')
- grad_bias_back: float32 [1024], P('row')
- grad_gain_two: float32 [1024], P('row')
- grad_shift_two: float32 [1024], P('row')
All inputs are finite; a program needn't handle non-finite values.
Results may differ from a plain program's by a relative error of at most 0.012.
The roundings to bfloat16 on the way count: a program that leaves them out, or rounds other values in their place, can miss the bound.
Values may be sent and summed in bfloat16 or wider, within the bound.
No kernel may reach another device: no remote copies, remote signals or barrier semaphores. Data moves between devices by JAX's collectives and lax.ppermute only.
A program may use at most 128 MiB of HBM per device.

v0:
```python
import jax
import jax.numpy as jnp
from jax import lax
from jax.sharding import PartitionSpec as P

HEAD_DIM = 64
SEQ_LEN = 512


norm_eps = 1e-12


def product_term(gathered, matrix, contract):
    return lax.dot_general(
        gathered, matrix, (((1,), (contract,)), ((), ())), preferred_element_type=jnp.float32
    )


def gather_cols(values):
    return lax.all_gather(values, "col", axis=0, tiled=True)


def gather_heads(values):
    return lax.all_gather(values, "row", axis=0, tiled=True)


def rows_sum(gathered, matrix, contract):
    return lax.psum_scatter(
        product_term(gathered, matrix, contract), "row", scatter_dimension=0, tiled=True
    )


def width_sum(gathered, matrix, contract):
    return lax.psum_scatter(
        product_term(gathered, matrix, contract), "col", scatter_dimension=0, tiled=True
    )


def pair_total(first_sum, second_sum):
    return lax.psum((first_sum, second_sum), "row")


def single_total(values):
    return lax.psum(values, "row")


def grad_pair(weight_grad, bias_grad):
    return lax.psum((weight_grad, bias_grad), "dp")


def normalize(resid):
    full_width = resid.shape[1] * lax.axis_size("row")
    row_mean = single_total(jnp.sum(resid, 1)) / full_width
    centered = resid - row_mean[:, None]
    variance = single_total(jnp.sum(centered * centered, 1)) / full_width
    inv_std = lax.rsqrt(variance + norm_eps)[:, None]
    return (centered * inv_std, inv_std)


def norm_backward(incoming, normed, inv_std, gain):
    full_width = incoming.shape[1] * lax.axis_size("row")
    scaled = incoming * gain.astype(jnp.float32)
    sum_plain, sum_cross = pair_total(jnp.sum(scaled, 1), jnp.sum(scaled * normed, 1))
    return inv_std * (
        scaled - sum_plain[:, None] / full_width - normed * (sum_cross[:, None] / full_width)
    )


def per_device(
    tokens,
    w_qkv,
    bias_qv,
    w_out,
    bias_out,
    gain_one,
    shift_one,
    w_in,
    bias_in,
    w_back,
    bias_back,
    gain_two,
    shift_two,
    cotangent,
):
    rows_width = tokens.shape[0]
    width_local = tokens.shape[1]
    heads_width = w_qkv.shape[2]
    rows_group = rows_width * lax.axis_size("col")
    rows_heads = rows_group // lax.axis_size("row")
    seq_count = rows_heads // SEQ_LEN
    head_count = heads_width // HEAD_DIM
    score_scale = HEAD_DIM ** (-0.5)
    seq_shape = (seq_count, SEQ_LEN, head_count, HEAD_DIM)
    qkv_matrix = jnp.transpose(w_qkv, (1, 0, 2)).reshape(width_local, 3 * heads_width)
    contract_rows = (((0,), (0,)), ((), ()))
    tokens_all = gather_cols(tokens)
    joined_rows = rows_sum(tokens_all, qkv_matrix, 0)
    queries = (joined_rows[:, :heads_width] + bias_qv[0]).astype(jnp.bfloat16).reshape(seq_shape)
    key_rows = joined_rows[:, heads_width : 2 * heads_width].astype(jnp.bfloat16).reshape(seq_shape)
    value_rows = (
        (joined_rows[:, 2 * heads_width :] + bias_qv[1]).astype(jnp.bfloat16).reshape(seq_shape)
    )
    scores = (
        jnp.einsum("sqhd,skhd->shqk", queries, key_rows, preferred_element_type=jnp.float32)
        * score_scale
    )
    row_peak = jnp.max(scores, -1, keepdims=True)
    expo_scores = jnp.exp(scores - row_peak)
    row_total = jnp.sum(expo_scores, -1, keepdims=True)
    attn_weights = expo_scores / row_total
    log_total = row_peak + jnp.log(row_total)
    context = jnp.einsum(
        "shqk,skhd->sqhd",
        attn_weights.astype(jnp.bfloat16),
        value_rows,
        preferred_element_type=jnp.float32,
    )
    context = context.reshape(rows_heads, heads_width).astype(jnp.bfloat16)
    context_all = gather_heads(context)
    attended = width_sum(context_all, w_out, 0) + bias_out
    resid_one = tokens.astype(jnp.float32) + attended
    normed_one, inv_one = normalize(resid_one)
    hidden_one = normed_one * gain_one + shift_one
    hidden_all = gather_cols(hidden_one.astype(jnp.bfloat16))
    pre_act = rows_sum(hidden_all, w_in, 0) + bias_in
    activated = jax.nn.gelu(pre_act, approximate=False).astype(jnp.bfloat16)
    activated_all = gather_heads(activated)
    mlp_out = width_sum(activated_all, w_back, 0) + bias_back
    resid_two = hidden_one + mlp_out
    normed_two, inv_two = normalize(resid_two)
    output = (normed_two * gain_two + shift_two).astype(jnp.bfloat16)
    grad_output = cotangent.astype(jnp.float32)
    grad_gain_two = jnp.sum(grad_output * normed_two, 0)
    grad_shift_two = jnp.sum(grad_output, 0)
    d_two = norm_backward(grad_output, normed_two, inv_two, gain_two)
    d_mlp_all = gather_cols(d_two.astype(jnp.bfloat16))
    grad_w_back = lax.dot_general(
        activated_all, d_mlp_all, contract_rows, preferred_element_type=jnp.float32
    )
    grad_bias_back = jnp.sum(d_mlp_all, 0, dtype=jnp.float32)
    grad_w_back, grad_bias_back = grad_pair(grad_w_back, grad_bias_back)
    d_activated = rows_sum(d_mlp_all, w_back, 1)
    normal_cdf = 0.5 * (1.0 + lax.erf(pre_act * 0.7071067811865476))
    normal_pdf = jnp.exp(-0.5 * pre_act * pre_act) * 0.3989422804014327
    d_pre = (d_activated * (normal_cdf + pre_act * normal_pdf)).astype(jnp.bfloat16)
    d_pre_all = gather_heads(d_pre)
    grad_w_in = lax.dot_general(
        hidden_all, d_pre_all, contract_rows, preferred_element_type=jnp.float32
    )
    grad_bias_in = jnp.sum(d_pre_all, 0, dtype=jnp.float32)
    grad_w_in, grad_bias_in = grad_pair(grad_w_in, grad_bias_in)
    d_hidden = d_two + width_sum(d_pre_all, w_in, 1)
    grad_gain_one = jnp.sum(d_hidden * normed_one, 0)
    grad_shift_one = jnp.sum(d_hidden, 0)
    d_one = norm_backward(d_hidden, normed_one, inv_one, gain_one)
    d_att_all = gather_cols(d_one.astype(jnp.bfloat16))
    grad_w_out = lax.dot_general(
        context_all, d_att_all, contract_rows, preferred_element_type=jnp.float32
    )
    grad_bias_out = jnp.sum(d_att_all, 0, dtype=jnp.float32)
    grad_w_out, grad_bias_out = grad_pair(grad_w_out, grad_bias_out)
    d_context = rows_sum(d_att_all, w_out, 1)
    d_context = d_context.astype(jnp.bfloat16).reshape(seq_shape)
    scores_again = (
        jnp.einsum("sqhd,skhd->shqk", queries, key_rows, preferred_element_type=jnp.float32)
        * score_scale
    )
    weights_again = jnp.exp(scores_again - log_total)
    d_value = jnp.einsum(
        "shqk,sqhd->skhd",
        weights_again.astype(jnp.bfloat16),
        d_context,
        preferred_element_type=jnp.float32,
    )
    d_weights = jnp.einsum(
        "sqhd,skhd->shqk", d_context, value_rows, preferred_element_type=jnp.float32
    )
    row_inner = jnp.sum(d_weights * weights_again, -1, keepdims=True)
    d_scores = (weights_again * (d_weights - row_inner)).astype(jnp.bfloat16)
    d_query = (
        jnp.einsum("shqk,skhd->sqhd", d_scores, key_rows, preferred_element_type=jnp.float32)
        * score_scale
    )
    d_key = (
        jnp.einsum("shqk,sqhd->skhd", d_scores, queries, preferred_element_type=jnp.float32)
        * score_scale
    )
    d_joined = jnp.concatenate(
        [
            d_query.reshape(rows_heads, heads_width),
            d_key.reshape(rows_heads, heads_width),
            d_value.reshape(rows_heads, heads_width),
        ],
        1,
    ).astype(jnp.bfloat16)
    d_joined_all = gather_heads(d_joined)
    grad_qkv_rows = lax.dot_general(
        tokens_all, d_joined_all, contract_rows, preferred_element_type=jnp.float32
    )
    grad_w_qkv = jnp.transpose(grad_qkv_rows.reshape(width_local, 3, heads_width), (1, 0, 2))
    grad_bias_qv = jnp.stack(
        [
            jnp.sum(d_joined_all[:, :heads_width], 0, dtype=jnp.float32),
            jnp.sum(d_joined_all[:, 2 * heads_width :], 0, dtype=jnp.float32),
        ]
    )
    grad_w_qkv, grad_bias_qv = grad_pair(grad_w_qkv, grad_bias_qv)
    grad_tokens = d_one + width_sum(d_joined_all, qkv_matrix, 1)
    grad_gain_one, grad_shift_one, grad_gain_two, grad_shift_two = lax.psum(
        (grad_gain_one, grad_shift_one, grad_gain_two, grad_shift_two), ("dp", "col")
    )
    return (
        output,
        grad_tokens,
        grad_w_qkv,
        grad_bias_qv,
        grad_w_out,
        grad_bias_out,
        grad_gain_one,
        grad_shift_one,
        grad_w_in,
        grad_bias_in,
        grad_w_back,
        grad_bias_back,
        grad_gain_two,
        grad_shift_two,
    )


def solution(mesh):
    in_specs = (
        P(("dp", "col"), "row"),
        P(None, "row", "col"),
        P(None, "col"),
        P("col", "row"),
        P("row"),
        P("row"),
        P("row"),
        P("row", "col"),
        P("col"),
        P("col", "row"),
        P("row"),
        P("row"),
        P("row"),
        P(("dp", "col"), "row"),
    )
    out_specs = (
        P(("dp", "col"), "row"),
        P(("dp", "col"), "row"),
        P(None, "row", "col"),
        P(None, "col"),
        P("col", "row"),
        P("row"),
        P("row"),
        P("row"),
        P("row", "col"),
        P("col"),
        P("col", "row"),
        P("row"),
        P("row"),
        P("row"),
    )
    return jax.shard_map(
        per_device, mesh=mesh, in_specs=in_specs, out_specs=out_specs, check_vma=False
    )
```

profile of v0, /device:TPU:0, one launch (start us, length us, event | category | flops | bytes accessed | tf_op | source)
XLA Modules:
  0.0 1359.5 jit_solution(17745313586469269785)
XLA Ops:
  9.1 49.1 %all-gather.9.cloned.1.call-done = bf16[4096,256]{1,0:T(8,128)(2,1)} async-done(((bf16[1024,256]{1,0:T(8,128)(2,1)}), bf16[4096,256]{1,0:T(8,128)(2,1)}) %all-gather.9.cloned.1.call-update) | async-done | bytes 2097168 | tf_op jit(solution)/shard_map/all_gather | solution.py:20
  58.3 8.0 fusion.53
  66.9 97.3 %reduce-scatter.9.cloned.1.call-done = f32[1024,768]{1,0:T(8,128)} async-done(((f32[4096,768]{1,0:T(8,128)}), f32[1024,768]{1,0:T(8,128)}) %reduce-scatter.9.cloned.1.call-update) | async-done | bytes 3145744 | tf_op jit(solution)/shard_map/reduce_scatter | solution.py:28
  178.5 22.7 %all-gather.11.cloned.1.call-done = bf16[4096,256]{0,1:T(8,128)(2,1)} async-done(((bf16[1024,256]{0,1:T(8,128)(2,1)}), bf16[4096,256]{0,1:T(8,128)(2,1)}) %all-gather.11.cloned.1.call-update) | async-done | bytes 2097168 | tf_op jit(solution)/shard_map/all_gather | solution.py:24
  207.8 74.6 %reduce-scatter.11.cloned.1.call-done = f32[1024,256]{1,0:T(8,128)} async-done(((f32[4096,256]{1,0:T(8,128)}), f32[1024,256]{1,0:T(8,128)}) %reduce-scatter.11.cloned.1.call-update) | async-done | bytes 1048592 | tf_op jit(solution)/shard_map/reduce_scatter | solution.py:34
  300.1 45.2 %all-gather.13.cloned.1.call-done = bf16[4096,256]{1,0:T(8,128)(2,1)} async-done(((bf16[1024,256]{1,0:T(8,128)(2,1)}), bf16[4096,256]{1,0:T(8,128)(2,1)}) %all-gather.13.cloned.1.call-update) | async-done | bytes 2097168 | tf_op jit(solution)/shard_map/all_gather | solution.py:20
  345.3 9.7 fusion.55
  355.6 124.3 %reduce-scatter.13.cloned.1.call-done = f32[1024,1024]{1,0:T(8,128)} async-done(((f32[4096,1024]{1,0:T(8,128)}), f32[1024,1024]{1,0:T(8,128)}) %reduce-scatter.13.cloned.1.call-update) | async-done | bytes 4194320 | tf_op jit(solution)/shard_map/reduce_scatter | solution.py:28
  479.9 11.4 fusion.6
  491.4 58.4 %all-gather.15.cloned.1.call-done = bf16[4096,1024]{1,0:T(8,128)(2,1)} async-done(((bf16[1024,1024]{1,0:T(8,128)(2,1)}), bf16[4096,1024]{1,0:T(8,128)(2,1)}) %all-gather.15.cloned.1.call-update) | async-done | bytes 8388624 | tf_op jit(solution)/shard_map/all_gather | solution.py:24
  549.8 7.7 fusion.56
  559.3 75.2 %reduce-scatter.15.cloned.1.call-done = f32[1024,256]{1,0:T(8,128)} async-done(((f32[4096,256]{1,0:T(8,128)}), f32[1024,256]{1,0:T(8,128)}) %reduce-scatter.15.cloned.1.call-update) | async-done | bytes 1048592 | tf_op jit(solution)/shard_map/reduce_scatter | solution.py:34
  667.7 46.0 %all-gather.17.cloned.1.call-done = bf16[4096,256]{1,0:T(8,128)(2,1)} async-done(((bf16[1024,256]{1,0:T(8,128)(2,1)}), bf16[4096,256]{1,0:T(8,128)(2,1)}) %all-gather.17.cloned.1.call-update) | async-done | bytes 2097168 | tf_op jit(solution)/shard_map/all_gather | solution.py:20
  713.7 9.7 fusion.57
  723.4 124.9 %reduce-scatter.17.cloned.1.call-done = f32[1024,1024]{1,0:T(8,128)} async-done(((f32[4096,1024]{1,0:T(8,128)}), f32[1024,1024]{1,0:T(8,128)}) %reduce-scatter.17.cloned.1.call-update) | async-done | bytes 4194320 | tf_op jit(solution)/shard_map/reduce_scatter | solution.py:28
  853.9 58.4 %all-gather.19.cloned.1.call-done = bf16[4096,1024]{1,0:T(8,128)(2,1)} async-done(((bf16[1024,1024]{1,0:T(8,128)(2,1)}), bf16[4096,1024]{1,0:T(8,128)(2,1)}) %all-gather.19.cloned.1.call-update) | async-done | bytes 8388624 | tf_op jit(solution)/shard_map/all_gather | solution.py:24
  912.3 7.7 fusion.58
  921.3 75.6 %reduce-scatter.19.cloned.1.call-done = f32[1024,256]{1,0:T(8,128)} async-done(((f32[4096,256]{1,0:T(8,128)}), f32[1024,256]{1,0:T(8,128)}) %reduce-scatter.19.cloned.1.call-update) | async-done | bytes 1048592 | tf_op jit(solution)/shard_map/reduce_scatter | solution.py:34
  1011.1 45.7 %all-gather.21.cloned.1.call-done = bf16[4096,256]{1,0:T(8,128)(2,1)} async-done(((bf16[1024,256]{1,0:T(8,128)(2,1)}), bf16[4096,256]{1,0:T(8,128)(2,1)}) %all-gather.21.cloned.1.call-update) | async-done | bytes 2097168 | tf_op jit(solution)/shard_map/all_gather | solution.py:20
  1061.7 42.7 %reduce-scatter.21.cloned.1.call-done = f32[1024,256]{1,0:T(8,128)} async-done(((f32[4096,256]{1,0:T(8,128)}), f32[1024,256]{1,0:T(8,128)}) %reduce-scatter.21.cloned.1.call-update) | async-done | bytes 1048592 | tf_op jit(solution)/shard_map/reduce_scatter | solution.py:28
  1124.5 46.5 %all-gather.23.cloned.1.call-done = bf16[4096,768]{0,1:T(8,128)(2,1)} async-done(((bf16[1024,768]{0,1:T(8,128)(2,1)}), bf16[4096,768]{0,1:T(8,128)(2,1)}) %all-gather.23.cloned.1.call-update) | async-done | bytes 6291472 | tf_op jit(solution)/shard_map/all_gather | solution.py:24
  1204.4 23.2 %all-reduce = (f32[256]{0:T(256)}, f32[256]{0:T(256)}, f32[256]{0:T(256)}, f32[256]{0:T(256)}) all-reduce(f32[256]{0:T(256)S(1)} %copy-done.28, f32[256]{0:T(256)S(1)} %copy-done.29, f32[256]{0:T(256)S(1)} %copy-done.31, f32[256]{0:T(256)S(1)} %copy-done.32), channel_id=1, replica_groups=mesh['dp'=2,'row'=4,'col'=4] {'dp','col'}, use_global_device_ids=true, to_apply=%region_35.0 | all-reduce | flops 1024 | bytes 8192 | tf_op jit(solution)/shard_map/psum | solution.py:209
  1236.7 18.5 %reduce-scatter.23.cloned.1.call-done = f32[1024,256]{1,0:T(8,128)} async-done(((f32[4096,256]{1,0:T(8,128)}), f32[1024,256]{1,0:T(8,128)}) %reduce-scatter.23.cloned.1.call-update) | async-done | bytes 1048592 | tf_op jit(solution)/shard_map/reduce_scatter | solution.py:34
  1257.8 87.6 %all-reduce.7.cloned.1.call-done = (f32[3,256,256]{2,1,0:T(8,128)}, f32[256,256]{1,0:T(8,128)}, f32[256,1024]{1,0:T(8,128)}, f32[1024,256]{1,0:T(8,128)}) async-done(((f32[3,256,256]{2,1,0:T(8,128)}, f32[256,256]{1,0:T(8,128)}, f32[256,1024]{1,0:T(8,128)}, f32[1024,256]{1,0:T(8,128)}), (f32[3,256,256]{2,1,0:T(8,128)}, f32[256,256]{1,0:T(8,128)}, f32[256,1024]{1,0:T(8,128)}, ...) | async-done | bytes 3145744 | tf_op jit(solution)/shard_map/psum | solution.py:48
  (202 shorter events, 174.8 us)
Async XLA Ops:
  7.2 542.6 %copy-start = (bf16[1024,256]{1,0:T(8,128)(2,1)S(1)}, bf16[1024,256]{1,0:T(8,128)(2,1)}, u32[]{:S(2)}) copy-start(bf16[1024,256]{1,0:T(8,128)(2,1)} %param.23) | copy-start | bytes 1572868
  7.2 51.1 %all-gather.9.cloned.1.call-start = ((), (), s32[]{:S(2)}) async-start(), calls=%async_computation.8 | async-start | bytes 2621440 | tf_op jit(solution)/shard_map/all_gather | solution.py:20
  7.9 156.3 %reduce-scatter.9.cloned.1.call-start = ((), (), s32[]{:S(2)}) async-start(), calls=%async_computation.9 | async-start | bytes 15728640 | tf_op jit(solution)/shard_map/reduce_scatter | solution.py:28
  66.3 134.9 %all-gather.11.cloned.1.call-start = ((), (), s32[]{:S(2)}) async-start(), calls=%async_computation.10 | async-start | bytes 2621440 | tf_op jit(solution)/shard_map/all_gather | solution.py:24
  178.4 104.0 %reduce-scatter.11.cloned.1.call-start = ((), (), s32[]{:S(2)}) async-start(), calls=%async_computation.11 | async-start | bytes 5242880 | tf_op jit(solution)/shard_map/reduce_scatter | solution.py:34
  205.4 77.0 %copy-start.13 = (bf16[1024,256]{1,0:T(8,128)(2,1)S(1)}, bf16[1024,256]{1,0:T(8,128)(2,1)}, u32[]{:S(2)}) copy-start(bf16[1024,256]{1,0:T(8,128)(2,1)} %param.14) | copy-start | bytes 1572868
  205.5 139.8 %copy-start.17 = (bf16[256,1024]{1,0:T(8,128)(2,1)S(1)}, bf16[256,1024]{1,0:T(8,128)(2,1)}, u32[]{:S(2)}) copy-start(bf16[256,1024]{1,0:T(8,128)(2,1)} %param.21) | copy-start | bytes 1572868
  205.5 139.8 %all-gather.13.cloned.1.call-start = ((), (), s32[]{:S(2)}) async-start(), calls=%async_computation.12 | async-start | bytes 2621440 | tf_op jit(solution)/shard_map/all_gather | solution.py:20
  299.6 180.4 %reduce-scatter.13.cloned.1.call-start = ((), (), s32[]{:S(2)}) async-start(), calls=%async_computation.13 | async-start | bytes 20971520 | tf_op jit(solution)/shard_map/reduce_scatter | solution.py:28
  355.0 194.8 %all-gather.15.cloned.1.call-start = ((), (), s32[]{:S(2)}) async-start(), calls=%async_computation.14 | async-start | bytes 10485760 | tf_op jit(solution)/shard_map/all_gather | solution.py:24
  355.6 135.7 %copy-start.27 = (f32[1024]{0:T(1024)}, f32[1024]{0:T(1024)S(1)}, u32[]{:S(2)}) copy-start(f32[1024]{0:T(1024)S(1)} %convert_element_type.106) | copy-start | bytes 12292
  491.3 143.1 %reduce-scatter.15.cloned.1.call-start = ((), (), s32[]{:S(2)}) async-start(), calls=%async_computation.15 | async-start | bytes 5242880 | tf_op jit(solution)/shard_map/reduce_scatter | solution.py:34
  557.5 156.2 %all-gather.17.cloned.1.call-start = ((), (), s32[]{:S(2)}) async-start(), calls=%async_computation.16 | async-start | bytes 2621440 | tf_op jit(solution)/shard_map/all_gather | solution.py:20
  667.4 180.9 %reduce-scatter.17.cloned.1.call-start = ((), (), s32[]{:S(2)}) async-start(), calls=%async_computation.17 | async-start | bytes 20971520 | tf_op jit(solution)/shard_map/reduce_scatter | solution.py:28
  723.4 188.9 %copy-start.18 = (bf16[256,1024]{1,0:T(8,128)(2,1)S(1)}, bf16[256,1024]{1,0:T(8,128)(2,1)}, u32[]{:S(2)}) copy-start(bf16[256,1024]{1,0:T(8,128)(2,1)} %param.21) | copy-start | bytes 1572868
  723.4 188.9 %all-gather.19.cloned.1.call-start = ((), (), s32[]{:S(2)}) async-start(), calls=%async_computation.18 | async-start | bytes 10485760 | tf_op jit(solution)/shard_map/all_gather | solution.py:24
  853.8 143.1 %reduce-scatter.19.cloned.1.call-start = ((), (), s32[]{:S(2)}) async-start(), calls=%async_computation.19 | async-start | bytes 5242880 | tf_op jit(solution)/shard_map/reduce_scatter | solution.py:34
  920.0 77.0 %copy-start.9 = (bf16[1024,256]{1,0:T(8,128)(2,1)S(1)}, bf16[1024,256]{1,0:T(8,128)(2,1)}, u32[]{:S(2)}) copy-start(bf16[1024,256]{1,0:T(8,128)(2,1)} %param.27) | copy-start | bytes 1572868
  920.0 136.7 %all-gather.21.cloned.1.call-start = ((), (), s32[]{:S(2)}) async-start(), calls=%async_computation.20 | async-start | bytes 2621440 | tf_op jit(solution)/shard_map/all_gather | solution.py:20
  1011.0 93.4 %reduce-scatter.21.cloned.1.call-start = ((), (), s32[]{:S(2)}) async-start(), calls=%async_computation.21 | async-start | bytes 5242880 | tf_op jit(solution)/shard_map/reduce_scatter | solution.py:28
  1061.0 110.0 %all-gather.23.cloned.1.call-start = ((), (), s32[]{:S(2)}) async-start(), calls=%async_computation.22 | async-start | bytes 7864320 | tf_op jit(solution)/shard_map/all_gather | solution.py:24
  1124.4 130.7 %reduce-scatter.23.cloned.1.call-start = ((), (), s32[]{:S(2)}) async-start(), calls=%async_computation.23 | async-start | bytes 5242880 | tf_op jit(solution)/shard_map/reduce_scatter | solution.py:34
  1177.6 167.9 %all-reduce.7.cloned.1.call-start = ((), (), s32[]{:S(2)}) async-start(), calls=%async_computation.24 | async-start | bytes 6291456 | tf_op jit(solution)/shard_map/psum | solution.py:48
  1255.1 97.4 %copy-start.1 = (bf16[1024,256]{1,0:T(8,128)(2,1)S(1)}, bf16[1024,256]{1,0:T(8,128)(2,1)}, u32[]{:S(2)}) copy-start(bf16[1024,256]{1,0:T(8,128)(2,1)} %param.23) | copy-start | bytes 1572868
  (36 other events, 316.6 us)
Sparse Core Ops, SparseCore 0:
  9.6 48.6 all-gather.8
  66.4 97.7 reduce-scatter.8
  178.5 22.5 all-gather.10
  205.6 76.7 reduce-scatter.10
  299.7 45.5 all-gather.12
  355.1 124.8 reduce-scatter.12
  491.5 58.2 all-gather.14
  557.6 76.7 reduce-scatter.14
  667.5 46.0 all-gather.16
  723.5 124.8 reduce-scatter.16
  853.9 58.2 all-gather.18
  920.1 76.7 reduce-scatter.18
  1011.1 45.5 all-gather.20
  1061.1 43.1 reduce-scatter.20
  1124.6 46.3 all-gather.22
  1177.7 77.3 reduce-scatter.22
  1258.7 86.6 all-reduce.6
where the time goes:
time: 1370 us; the launch traced here: 1360 us
  waiting for transfers between devices  1090 us (80%)
  matrix products  90.1 us (7%)
  blocking collectives  69.4 us (5%)
  other arithmetic  63.7 us (5%)
  local copies, waits for them, and re-layouts  26 us (2%)
  between operations  14.9 us (1%)
    reduce_scatter x4, waiting for transfers between devices, rows_sum(): lax.psum_scatter(product_term(gathered, matrix, contract), 'row', scatter...  389 us
    reduce_scatter x4, waiting for transfers between devices, width_sum(): lax.psum_scatter(product_term(gathered, matrix, contract), 'col', scatter...  244 us
    all_gather x4, waiting for transfers between devices, gather_heads(): return lax.all_gather(values, 'row', axis=0, tiled=True)  186 us
    all_gather x4, waiting for transfers between devices, gather_cols(): return lax.all_gather(values, 'col', axis=0, tiled=True)  186 us
    psum x1, waiting for transfers between devices, grad_pair(): return lax.psum((weight_grad, bias_grad), 'dp')  87.6 us
    dot_general x8, matrix products, product_term(): lax.dot_general(gathered, matrix, (((1,), (contract,)), ((), ())), prefer...  57.8 us
  transfers between devices with their start and end apart: 17, of which 17 were waited for; matrix products, arithmetic and copies ran while one was open for 3% of the time, Pallas kernels for 0%

commit v1 on v0

v1 whole, which is shorter than its diff:
```python
import jax
import jax.numpy as jnp
from jax import lax
from jax.sharding import PartitionSpec as P

HEAD_DIM = 64
SEQ_LEN = 512
norm_eps = 1e-12

f32 = jnp.float32
bf16 = jnp.bfloat16


def swap(values, axis, bit):
    size = lax.axis_size(axis)
    return lax.ppermute(values, axis, [(i, i ^ bit) for i in range(size)])


def dot(left, right, left_dim, right_dim):
    return lax.dot_general(
        left, right, (((left_dim,), (right_dim,)), ((), ())), preferred_element_type=f32
    )


def row_gather(block):
    across = swap(block, "row", 2)
    beside = swap(block, "row", 1)
    return [block, beside, across, swap(across, "row", 1)]


def row_reduce(parts):
    far = parts[2] + swap(parts[3].astype(bf16), "row", 1).astype(f32)
    far = swap(far.astype(bf16), "row", 2).astype(f32)
    near = parts[0] + swap(parts[1].astype(bf16), "row", 1).astype(f32)
    return near + far


def col_gather(block):
    size = lax.axis_size("col")
    here = lax.axis_index("col")
    up, down = [block], [block]
    for step in range(1, size):
        up.append(lax.ppermute(up[-1], "col", [(i, i - 1) for i in range(1, size - step + 1)]))
        down.append(lax.ppermute(down[-1], "col", [(i, i + 1) for i in range(step - 1, size - 1)]))
    return [block] + [
        jnp.where(here + step < size, up[step], down[size - step]) for step in range(1, size)
    ]


def col_reduce(parts):
    size = lax.axis_size("col")
    up = down = None
    for step in range(1, size):
        send_down, send_up = parts[size - step].astype(f32), parts[step].astype(f32)
        if step > 1:
            send_down, send_up = send_down + down.astype(f32), send_up + up.astype(f32)
        down = lax.ppermute(send_down.astype(bf16), "col", [(i, i + 1) for i in range(step)])
        up = lax.ppermute(
            send_up.astype(bf16), "col", [(i, i - 1) for i in range(size - step, size)]
        )
    return parts[0].astype(f32) + down.astype(f32) + up.astype(f32)


def dp_sum(values):
    size = lax.axis_size("dp")
    bit = 1
    while bit < size:
        low = values.astype(bf16)
        values = low.astype(f32) + swap(low, "dp", bit).astype(f32)
        bit *= 2
    return values


def normalize(resid):
    row_mean = jnp.mean(resid, 1, keepdims=True)
    centered = resid - row_mean
    variance = jnp.mean(centered * centered, 1, keepdims=True)
    inv_std = lax.rsqrt(variance + norm_eps)
    return centered * inv_std, inv_std


def norm_backward(incoming, normed, inv_std, gain):
    scaled = incoming * gain
    return inv_std * (
        scaled
        - jnp.mean(scaled, 1, keepdims=True)
        - normed * jnp.mean(scaled * normed, 1, keepdims=True)
    )


def row_swap(values, split, concat):
    return lax.all_to_all(values, "row", split, concat, tiled=True)


def per_device(
    tokens,
    w_qkv,
    bias_qv,
    w_out,
    bias_out,
    gain_one,
    shift_one,
    w_in,
    bias_in,
    w_back,
    bias_back,
    gain_two,
    shift_two,
    cotangent,
):
    rows, cols = lax.axis_size("row"), lax.axis_size("col")
    r, c = lax.axis_index("row"), lax.axis_index("col")
    group, width_local = tokens.shape
    block = group // rows
    width = width_local * rows
    heads_tile = w_qkv.shape[2]
    head_piece = heads_tile // rows
    hid_tile = w_in.shape[1]
    hid_piece = hid_tile // rows
    seq_count = group // SEQ_LEN
    head_count = cols * head_piece // HEAD_DIM
    score_scale = HEAD_DIM ** (-0.5)
    seq_shape = (seq_count, SEQ_LEN, head_count, HEAD_DIM)

    wq = jnp.transpose(w_qkv, (2, 0, 1)).reshape(rows, head_piece, 3, width_local)
    wq = jnp.transpose(wq, (0, 2, 1, 3)).reshape(rows * 3 * head_piece, width_local)
    wq = row_swap(wq, 0, 1)
    wq_blocks = [b.reshape(3, 1, head_piece, width) for b in col_gather(wq)]
    wq_all = jnp.concatenate(wq_blocks, 1).reshape(3 * cols * head_piece, width)

    across = swap(tokens, "row", 2)
    low_y = (r & 2) == 0
    pair = jnp.concatenate(
        [jnp.where(low_y, tokens, across), jnp.where(low_y, across, tokens)], 1
    )
    other = swap(pair, "row", 1)
    low_core = (r & 1) == 0
    even, odd = jnp.where(low_core, pair, other), jnp.where(low_core, other, pair)
    tokens_all = jnp.concatenate(
        [even[:, :width_local], odd[:, :width_local], even[:, width_local:], odd[:, width_local:]],
        1,
    )

    vectors = jnp.stack([bias_out, gain_one, shift_one, bias_back, gain_two, shift_two])
    vectors = lax.all_gather(vectors, "row", axis=1, tiled=True).astype(f32)
    bias_out_f, gain_one_f, shift_one_f, bias_back_f, gain_two_f, shift_two_f = [
        vectors[i] for i in range(6)
    ]
    hid_bias = lax.dynamic_slice(bias_in, (r * hid_piece,), (hid_piece,))
    head_bias = lax.dynamic_slice(bias_qv, (0, r * head_piece), (2, head_piece)).reshape(-1)
    col_bias = lax.all_gather(jnp.concatenate([hid_bias, head_bias]), "col", axis=0)
    col_bias = jnp.concatenate([col_bias, col_bias])
    col_bias = lax.dynamic_slice(col_bias, (c, 0), (cols, col_bias.shape[1])).astype(f32)
    bias_in_f = col_bias[:, :hid_piece].reshape(-1)
    bias_q = col_bias[:, hid_piece : hid_piece + head_piece].reshape(-1)
    bias_v = col_bias[:, hid_piece + head_piece :].reshape(-1)

    wo = row_swap(w_out, 0, 1)
    wo_all = jnp.concatenate(col_gather(wo), 0)
    wi = row_swap(w_in, 1, 0)
    wi_all = jnp.concatenate(col_gather(wi), 1)
    wb = row_swap(w_back, 0, 1)
    wb_all = jnp.concatenate(col_gather(wb), 0)
    cot = row_swap(cotangent, 0, 1).astype(f32)

    heads_width = cols * head_piece
    joined = dot(tokens_all, wq_all, 1, 1)
    queries = (joined[:, :heads_width] + bias_q).astype(bf16).reshape(seq_shape)
    key_rows = joined[:, heads_width : 2 * heads_width].astype(bf16).reshape(seq_shape)
    value_rows = (joined[:, 2 * heads_width :] + bias_v).astype(bf16).reshape(seq_shape)
    scores = (
        jnp.einsum("sqhd,skhd->shqk", queries, key_rows, preferred_element_type=f32) * score_scale
    )
    row_peak = jnp.max(scores, -1, keepdims=True)
    expo_scores = jnp.exp(scores - row_peak)
    row_total = jnp.sum(expo_scores, -1, keepdims=True)
    attn_weights = expo_scores / row_total
    log_total = row_peak + jnp.log(row_total)
    context = jnp.einsum(
        "shqk,skhd->sqhd", attn_weights.astype(bf16), value_rows, preferred_element_type=f32
    )
    context = context.reshape(group, heads_width).astype(bf16)

    def token_blocks(values):
        return [
            lax.dynamic_slice(values, ((r ^ j) * block, 0), (block, values.shape[1]))
            for j in range(rows)
        ]

    attended = row_reduce([dot(b, wo_all, 1, 0) for b in token_blocks(context)]) + bias_out_f
    tokens_own = lax.dynamic_slice(tokens_all, (r * block, 0), (block, width)).astype(f32)
    normed_one, inv_one = normalize(tokens_own + attended)
    hidden_one = normed_one * gain_one_f + shift_one_f

    hidden_all = jnp.concatenate(row_gather(hidden_one.astype(bf16)), 0)
    pre_act = dot(hidden_all, wi_all, 1, 0) + bias_in_f
    normal_cdf = 0.5 * (1.0 + lax.erf(pre_act * 0.7071067811865476))
    activated = (pre_act * normal_cdf).astype(bf16)
    mlp = dot(activated, wb_all, 1, 0)
    mlp_out = row_reduce([mlp[j * block : (j + 1) * block] for j in range(rows)]) + bias_back_f
    normed_two, inv_two = normalize(hidden_one + mlp_out)
    output = row_swap((normed_two * gain_two_f + shift_two_f).astype(bf16), 1, 0)

    d_two = norm_backward(cot, normed_two, inv_two, gain_two_f)
    d_mlp = d_two.astype(bf16)
    d_mlp_all = jnp.concatenate(row_gather(d_mlp), 0)
    d_activated = dot(d_mlp_all, wb_all, 1, 1)
    normal_pdf = jnp.exp(-0.5 * pre_act * pre_act) * 0.3989422804014327
    d_pre = (d_activated * (normal_cdf + pre_act * normal_pdf)).astype(bf16)
    d_hid = dot(d_pre, wi_all, 1, 1)
    d_hidden = d_two + row_reduce([d_hid[j * block : (j + 1) * block] for j in range(rows)])

    grad_wb = dot(activated, d_mlp_all, 0, 0).astype(bf16)
    grad_wb = dp_sum(
        col_reduce([grad_wb[d * hid_piece : (d + 1) * hid_piece] for d in range(cols)])
    )
    grad_w_back = row_swap(grad_wb.astype(bf16), 1, 0).astype(f32)
    grad_wi = dot(hidden_all, d_pre, 0, 0).astype(bf16)
    grad_wi = dp_sum(
        col_reduce([grad_wi[:, d * hid_piece : (d + 1) * hid_piece] for d in range(cols)])
    )
    grad_w_in = row_swap(grad_wi.astype(bf16), 0, 1).astype(f32)

    d_one = norm_backward(d_hidden, normed_one, inv_one, gain_one_f)
    d_att = d_one.astype(bf16)
    d_att_blocks = row_gather(d_att)
    d_att_rel = jnp.concatenate(d_att_blocks, 0)

    def by_position(blocks):
        joint = jnp.concatenate(blocks, 0).reshape(rows, block, -1)
        return jnp.take(joint, r ^ jnp.arange(rows), axis=0).reshape(group, -1)

    d_one_cols = row_swap(d_one, 1, 0)
    d_att_all = by_position(d_att_blocks)
    grad_wo = dot(context, d_att_all, 0, 0).astype(bf16)
    grad_wo = dp_sum(
        col_reduce([grad_wo[d * head_piece : (d + 1) * head_piece] for d in range(cols)])
    )
    grad_w_out = row_swap(grad_wo.astype(bf16), 1, 0).astype(f32)

    vector_grads = jnp.stack(
        [
            jnp.sum(d_att, 0, dtype=f32),
            jnp.sum(d_hidden * normed_one, 0),
            jnp.sum(d_hidden, 0),
            jnp.sum(d_mlp, 0, dtype=f32),
            jnp.sum(cot * normed_two, 0),
            jnp.sum(cot, 0),
        ]
    )

    def from_col(values):
        doubled = jnp.concatenate([values, values])
        start = (cols - c) % cols
        return lax.dynamic_slice_in_dim(doubled, start, cols, 0)

    hid_sums = from_col(jnp.sum(d_pre, 0, dtype=f32).reshape(cols, 1, hid_piece))
    hid_sums = jnp.where(jnp.arange(rows)[None, :, None] == r, hid_sums, 0.0)
    vector_grads, hid_sums = lax.psum((vector_grads, hid_sums), ("dp", "row", "col"))
    vector_grads = lax.dynamic_slice(vector_grads, (0, r * width_local), (6, width_local))
    grad_bias_in = lax.dynamic_slice_in_dim(hid_sums, c, 1, 0).reshape(hid_tile)

    d_context = dot(d_att_all, wo_all, 1, 1).astype(bf16).reshape(seq_shape)
    scores_again = (
        jnp.einsum("sqhd,skhd->shqk", queries, key_rows, preferred_element_type=f32) * score_scale
    )
    weights_again = jnp.exp(scores_again - log_total)
    d_value = jnp.einsum(
        "shqk,sqhd->skhd", weights_again.astype(bf16), d_context, preferred_element_type=f32
    )
    d_weights = jnp.einsum("sqhd,skhd->shqk", d_context, value_rows, preferred_element_type=f32)
    row_inner = jnp.sum(d_weights * weights_again, -1, keepdims=True)
    d_scores = (weights_again * (d_weights - row_inner)).astype(bf16)
    d_query = (
        jnp.einsum("shqk,skhd->sqhd", d_scores, key_rows, preferred_element_type=f32) * score_scale
    )
    d_key = (
        jnp.einsum("shqk,sqhd->skhd", d_scores, queries, preferred_element_type=f32) * score_scale
    )
    d_joined = jnp.concatenate(
        [
            d_query.reshape(group, heads_width),
            d_key.reshape(group, heads_width),
            d_value.reshape(group, heads_width),
        ],
        1,
    ).astype(bf16)
    grad_wq = dot(d_joined, tokens_all, 0, 0).astype(bf16)
    grad_wq = grad_wq.reshape(3, cols, head_piece, width)
    grad_wq = dp_sum(
        col_reduce([grad_wq[:, d].reshape(3 * head_piece, width) for d in range(cols)])
    )
    grad_wq = row_swap(grad_wq.astype(bf16), 1, 0).reshape(rows, 3, head_piece, width_local)
    grad_w_qkv = jnp.transpose(grad_wq, (1, 3, 0, 2)).reshape(3, width_local, heads_tile)
    grad_w_qkv = grad_w_qkv.astype(f32)

    d_tokens = dot(d_joined, wq_all, 1, 0)
    d_tokens = row_reduce(
        [
            lax.dynamic_slice(d_tokens, (0, (r ^ j) * width_local), (group, width_local))
            for j in range(rows)
        ]
    )
    grad_tokens = d_one_cols + d_tokens

    head_sums = jnp.stack(
        [
            jnp.sum(d_joined[:, :heads_width], 0, dtype=f32),
            jnp.sum(d_joined[:, 2 * heads_width :], 0, dtype=f32),
        ],
    ).reshape(2, cols, head_piece)
    head_sums = from_col(jnp.transpose(head_sums, (1, 0, 2))[:, :, None, :])
    head_sums = jnp.where(jnp.arange(rows)[None, None, :, None] == r, head_sums, 0.0)
    head_sums = lax.psum(head_sums, ("dp", "row", "col"))
    grad_bias_qv = lax.dynamic_slice_in_dim(head_sums, c, 1, 0).reshape(2, heads_tile)

    return (
        output,
        grad_tokens,
        grad_w_qkv,
        grad_bias_qv,
        grad_w_out,
        vector_grads[0],
        vector_grads[1],
        vector_grads[2],
        grad_w_in,
        grad_bias_in,
        grad_w_back,
        vector_grads[3],
        vector_grads[4],
        vector_grads[5],
    )


def solution(mesh):
    in_specs = (
        P(("dp", "col"), "row"),
        P(None, "row", "col"),
        P(None, "col"),
        P("col", "row"),
        P("row"),
        P("row"),
        P("row"),
        P("row", "col"),
        P("col"),
        P("col", "row"),
        P("row"),
        P("row"),
        P("row"),
        P(("dp", "col"), "row"),
    )
    out_specs = (
        P(("dp", "col"), "row"),
        P(("dp", "col"), "row"),
        P(None, "row", "col"),
        P(None, "col"),
        P("col", "row"),
        P("row"),
        P("row"),
        P("row"),
        P("row", "col"),
        P("col"),
        P("col", "row"),
        P("row"),
        P("row"),
        P("row"),
    )
    return jax.shard_map(
        per_device, mesh=mesh, in_specs=in_specs, out_specs=out_specs, check_vma=False
    )
```

time: 1370 us -> 553 us (0.40)
  waiting for transfers between devices: 1090 us -> 146 us
  starting transfers between devices: 1.8 us -> 166 us
  matrix products: 90.1 us -> 61.9 us
  local copies, waits for them, and re-layouts: 26 us -> 51.3 us
    reduce_scatter x8 -> x0, waiting for transfers between devices: 633 us -> none  [the longest x4 389 us: rows_sum(): lax.psum_scatter(product_term(gathered, matrix, contract), 'row', scatter...]
    all_gather x8 -> x0, waiting for transfers between devices: 372 us -> none  [the longest x4 186 us: gather_heads(): return lax.all_gather(values, 'row', axis=0, tiled=True)]
    ppermute x0 -> x75, starting transfers between devices: none -> 127 us  [the longest x12 53.5 us: col_reduce(): lax.ppermute(send_down.astype(bf16), 'col', [(i, i + 1) for i in range(st...]
    ppermute x0 -> x75, waiting for transfers between devices: none -> 110 us  [the longest x12 55.2 us: col_gather(): lax.ppermute(up[-1], 'col', [(i, i - 1) for i in range(1, size - step + 1)])]
    psum x1 -> x0, waiting for transfers between devices: 87.6 us -> none  [grad_pair(): return lax.psum((weight_grad, bias_grad), 'dp')]
    all_to_all x0 -> x11, starting transfers between devices: none -> 39.7 us  [row_swap(): return lax.all_to_all(values, 'row', split, concat, tiled=True)]
    all_to_all x0 -> x11, waiting for transfers between devices: none -> 35.2 us  [row_swap(): return lax.all_to_all(values, 'row', split, concat, tiled=True)]
    dot_general x16 -> x19, matrix products: 84.6 us -> 56.4 us  [the longest x15 46.6 us: dot(): lax.dot_general(left, right, (((left_dim,), (right_dim,)), ((), ())), pre...]
  transfers between devices with their start and end apart: 17 -> 86, of which waited for: 17 -> 25; matrix products, arithmetic and copies ran while one was open for 3% -> 25% of each run, Pallas kernels for 0% -> 0%
where the time goes in v1:
time: 553 us; the launch traced here: 546 us
  starting transfers between devices  166 us (30%)
  waiting for transfers between devices  146 us (26%)
  matrix products  61.9 us (11%)
  blocking collectives  59.8 us (11%)
  other arithmetic  57.9 us (10%)
  local copies, waits for them, and re-layouts  51.3 us (9%)
    ppermute x12, waiting for transfers between devices, col_gather(): lax.ppermute(up[-1], 'col', [(i, i - 1) for i in range(1, size - step + 1)])  55.2 us
    ppermute x12, starting transfers between devices, col_reduce(): lax.ppermute(send_down.astype(bf16), 'col', [(i, i + 1) for i in range(st...  53.5 us
    dot_general x15, matrix products, dot(): lax.dot_general(left, right, (((left_dim,), (right_dim,)), ((), ())), pre...  46.6 us
    psum x1, blocking collectives, per_device(): head_sums = lax.psum(head_sums, ('dp', 'row', 'col'))  41.7 us
    all_to_all x11, starting transfers between devices, row_swap(): return lax.all_to_all(values, 'row', split, concat, tiled=True)  39.7 us
    all_to_all x11, waiting for transfers between devices, row_swap(): return lax.all_to_all(values, 'row', split, concat, tiled=True)  35.2 us
    ppermute x27, waiting for transfers between devices, swap(): return lax.ppermute(values, axis, [(i, i ^ bit) for i in range(size)])  34.9 us
    ppermute x12, starting transfers between devices, col_gather(): lax.ppermute(down[-1], 'col', [(i, i + 1) for i in range(step - 1, size -...  24.7 us
  transfers between devices with their start and end apart: 86, of which 25 were waited for; matrix products, arithmetic and copies ran while one was open for 25% of the time, Pallas kernels for 0%

profile of v1, /device:TPU:0, one launch (start us, length us, event | category | flops | bytes accessed | tf_op | source)
XLA Modules:
  0.0 546.1 jit_solution(14062031612441579460)
XLA Ops:
  15.3 5.4 all-to-all-done
  33.0 12.8 %all-gather.1 = bf16[4,1,384]{2,1,0:T(2,128)(2,1)S(1)} all-gather(bf16[1,1,384]{2,1,0:T(2,128)(2,1)S(1)} %reshape.312), channel_id=2, replica_groups=mesh['dp'=2,'row'=4,'col'=4] {'col'}, dimensions={0}, use_global_device_ids=true | all-gather | bytes 3840 | tf_op jit(solution)/shard_map/all_gather | solution.py:151
  56.2 6.0 %collective-permute-start.3 = (bf16[192,1024]{1,0:T(8,128)(2,1)S(1)}, bf16[192,1024]{1,0:T(8,128)(2,1)}, u32[]{:S(2)}, u32[]{:S(2)}) collective-permute-start(bf16[192,1024]{1,0:T(8,128)(2,1)S(1)} %bitcast.226), channel_id=1, source_target_pairs={{0,1},{1,2},{2,3},{4,5},{5,6},{6,7},{8,9},{9,10},{10,11},{12,13},{... | collective-permute-start | bytes 1179656 | tf_op jit(solution)/shard_map/ppermute | solution.py:44
  69.0 9.2 %collective-permute-done.13 = bf16[64,1024]{1,0:T(8,128)(2,1)S(1)} collective-permute-done((bf16[64,1024]{1,0:T(8,128)(2,1)}, bf16[64,1024]{1,0:T(8,128)(2,1)S(1)}, u32[]{:S(2)}, u32[]{:S(2)}) %collective-permute-start.13) | collective-permute-done | bytes 131104 | tf_op jit(solution)/shard_map/ppermute | solution.py:43
  86.2 18.7 %collective-permute-done.6 = bf16[192,1024]{1,0:T(8,128)(2,1)S(1)} collective-permute-done((bf16[192,1024]{1,0:T(8,128)(2,1)}, bf16[192,1024]{1,0:T(8,128)(2,1)S(1)}, u32[]{:S(2)}, u32[]{:S(2)}) %collective-permute-start.6) | collective-permute-done | bytes 393248 | tf_op jit(solution)/shard_map/ppermute | solution.py:43
  106.3 5.4 collective-permute-start.27
  135.4 5.3 all_gather.11
  151.0 13.9 %collective-permute-done.30 = bf16[256,1024]{0,1:T(8,128)(2,1)S(1)} collective-permute-done((bf16[256,1024]{0,1:T(8,128)(2,1)}, bf16[256,1024]{0,1:T(8,128)(2,1)S(1)}, u32[]{:S(2)}, u32[]{:S(2)}) %collective-permute-start.30) | collective-permute-done | bytes 524320 | tf_op jit(solution)/shard_map/ppermute | solution.py:43
  170.5 5.6 %collective-permute-done.25 = bf16[1024,256]{1,0:T(8,128)(2,1)S(1)} collective-permute-done((bf16[1024,256]{1,0:T(8,128)(2,1)}, bf16[1024,256]{1,0:T(8,128)(2,1)S(1)}, u32[]{:S(2)}, u32[]{:S(2)}) %collective-permute-start.25) | collective-permute-done | bytes 524320 | tf_op jit(solution)/shard_map/ppermute | solution.py:43
  187.9 6.1 %multiply_convert_fusion.1 = (bf16[1024,1024]{1,0:T(8,128)(2,1)S(1)}, f32[1024,1024]{1,0:T(8,128)}) fusion(f32[1024]{0:T(1024)S(1)} %bitcast.261, bf16[1024,256]{1,0:T(8,128)(2,1)S(1)} %broadcast_select_fusion.6, bf16[1024,256]{1,0:T(8,128)(2,1)S(1)} %broadcast_select_fusion.7, bf16[1024,256]{1,0:T(8,128)(2,1)S(1)} %broadcast_select_fusion.8, ...), kind=kOutput, calls=%fused_computation.19 | convolution fusion | flops 2170552320 | bytes 10489856 | tf_op jit(solution)/shard_map/dot_general | solution.py:20
  194.0 5.8 %fusion.94 = (bf16[1024,1024]{1,0:T(8,128)(2,1)S(1)}, f32[1024,1024]{1,0:T(8,128)}) fusion(bf16[1024,1024]{1,0:T(8,128)(2,1)S(1)} %get-tuple-element.135, bf16[256,1024]{0,1:T(8,128)(2,1)S(1)} %broadcast_select_fusion.3, bf16[256,1024]{0,1:T(8,128)(2,1)S(1)} %broadcast_select_fusion.4, bf16[256,1024]{0,1:T(8,128)(2,1)S(1)} %broadcast_select_fusion.5, ...), kind=kOutput, calls=%fused_computation.231 | convolution fusion | flops 2156920832 | bytes 10485760 | tf_op jit(solution)/shard_map/dot_general | solution.py:20
  214.1 10.4 %collective-permute-done.34 = bf16[256,1024]{1,0:T(8,128)(2,1)} collective-permute-done((bf16[256,1024]{1,0:T(8,128)(2,1)}, bf16[256,1024]{1,0:T(8,128)(2,1)}, u32[]{:S(2)}, u32[]{:S(2)}) %collective-permute-start.34) | collective-permute-done | bytes 524320 | tf_op jit(solution)/shard_map/ppermute | solution.py:16
  228.7 13.4 %collective-permute-done.36 = bf16[256,1024]{1,0:T(8,128)(2,1)} collective-permute-done((bf16[256,1024]{1,0:T(8,128)(2,1)}, bf16[256,1024]{1,0:T(8,128)(2,1)}, u32[]{:S(2)}, u32[]{:S(2)}) %collective-permute-start.36) | collective-permute-done | bytes 524320 | tf_op jit(solution)/shard_map/ppermute | solution.py:16
  247.3 8.8 %all-to-all-done.4 = bf16[256,4,256]{2,0,1:T(8,128)(2,1)} async-done(((bf16[256,4,256]{2,0,1:T(8,128)(2,1)}), bf16[256,4,256]{2,0,1:T(8,128)(2,1)}, u32[]{:S(2)}, u32[]{:S(2)}) %all-to-all-start.4) | async-done | bytes 524320 | tf_op jit(solution)/shard_map/all_to_all | solution.py:92
  263.1 6.4 %collective-permute-start.68 = (bf16[256,1024]{0,1:T(8,128)(2,1)}, bf16[256,1024]{0,1:T(8,128)(2,1)}, u32[]{:S(2)}, u32[]{:S(2)}) collective-permute-start(bf16[256,1024]{0,1:T(8,128)(2,1)} %get-tuple-element.84), channel_id=1, source_target_pairs={{0,1},{4,5},{8,9},{12,13},{16,17},{20,21},{24,25},{28,29}} | collective-permute-start | bytes 1572872 | tf_op jit(solution)/shard_map/ppermute | solution.py:57
  271.5 5.3 convert_reduce_fusion
  276.9 5.6 %fusion.95 = (bf16[1024,1024]{1,0:T(8,128)(2,1)S(1)}, f32[1024,1024]{1,0:T(8,128)}) fusion(bf16[1024,1024]{1,0:T(8,128)(2,1)S(1)} %get-tuple-element.144, bf16[1024,256]{1,0:T(8,128)(2,1)S(1)} %copy-done.35, bf16[1024,256]{1,0:T(8,128)(2,1)S(1)} %copy-done.29, bf16[1024,256]{1,0:T(8,128)(2,1)S(1)} %copy-done.37, bf16[1024,256]{1,0:T(8,128)(2,1)} %bitcast.17), kind=kOutput, calls=%fused_computation.232 | convolution fusion | flops 2156920832 | bytes 10485760 | tf_op jit(solution)/shard_map/dot_general | solution.py:20
  315.4 6.6 %collective-permute-start.70 = (bf16[256,1024]{0,1:T(8,128)(2,1)}, bf16[256,1024]{0,1:T(8,128)(2,1)}, u32[]{:S(2)}, u32[]{:S(2)}) collective-permute-start(bf16[256,1024]{0,1:T(8,128)(2,1)} %get-tuple-element.80), channel_id=1, source_target_pairs={{0,1},{1,2},{2,3},{4,5},{5,6},{6,7},{8,9},{9,10},{10,11},{12,13},{... | collective-permute-start | bytes 1572872 | tf_op jit(solution)/shard_map/ppermute | solution.py:57
  326.4 8.2 %collective-permute-start.63 = (bf16[1024,256]{1,0:T(8,128)(2,1)S(1)}, bf16[1024,256]{1,0:T(8,128)(2,1)S(1)}, u32[]{:S(2)}, u32[]{:S(2)}) collective-permute-start(bf16[1024,256]{1,0:T(8,128)(2,1)S(1)} %get-tuple-element.86), channel_id=1, source_target_pairs={{0,1},{1,2},{2,3},{4,5},{5,6},{6,7},{8,9},{9,10},{10,11},{12,13},{... | collective-permute-start | bytes 1572872 | tf_op jit(solution)/shard_map/ppermute | solution.py:57
  346.9 5.7 %collective-permute-done.66 = bf16[1024,256]{1,0:T(8,128)(2,1)} collective-permute-done((bf16[1024,256]{1,0:T(8,128)(2,1)S(1)}, bf16[1024,256]{1,0:T(8,128)(2,1)}, u32[]{:S(2)}, u32[]{:S(2)}) %collective-permute-start.66) | collective-permute-done | bytes 524320 | tf_op jit(solution)/shard_map/ppermute | solution.py:58
  365.3 5.1 fusion.26
  406.1 41.7 %all-reduce = (f32[4,2,4,64]{3,2,1,0:T(4,128)}, f32[6,1024]{1,0:T(8,128)}, f32[4,4,256]{2,1,0:T(4,128)}) all-reduce(f32[4,2,4,64]{3,2,1,0:T(4,128)} %broadcast_select_fusion.18, f32[6,1024]{1,0:T(8,128)} %stack.67, f32[4,4,256]{2,1,0:T(4,128)} %broadcast_select_fusion.17), channel_id=1, replica_groups=mesh['dp'=2,'row'=4,'col'=4] {'dp','row','col'}, use_global_device_ids=true, to_apply=%region_13.14 | all-reduce | flops 12288 | bytes 98304 | tf_op jit(solution)/shard_map/psum | solution.py:314
  460.0 6.3 %collective-permute-start.56 = (bf16[64,1024]{1,0:T(8,128)(2,1)S(1)}, bf16[64,1024]{1,0:T(8,128)(2,1)S(1)}, u32[]{:S(2)}, u32[]{:S(2)}) collective-permute-start(bf16[64,1024]{1,0:T(8,128)(2,1)S(1)} %get-tuple-element.109), channel_id=1, source_target_pairs={{0,1},{1,2},{2,3},{4,5},{5,6},{6,7},{8,9},{9,10},{10,11},{12,13},{... | collective-permute-start | bytes 393224 | tf_op jit(solution)/shard_map/ppermute | solution.py:57
  519.6 6.5 %collective-permute-done.53 = bf16[192,1024]{1,0:T(8,128)(2,1)} collective-permute-done((bf16[192,1024]{1,0:T(8,128)(2,1)S(1)}, bf16[192,1024]{1,0:T(8,128)(2,1)}, u32[]{:S(2)}, u32[]{:S(2)}) %collective-permute-start.53) | collective-permute-done | bytes 393248 | tf_op jit(solution)/shard_map/ppermute | solution.py:16
  (484 shorter events, 318.8 us)
Async XLA Ops:
  20.6 27.9 %all-to-all-start.2 = ((bf16[256,4,256]{0,2,1:T(8,128)(2,1)}), bf16[256,4,256]{0,2,1:T(8,128)(2,1)S(1)}, u32[]{:S(2)}, u32[]{:S(2)}) async-start(bf16[256,4,256]{0,2,1:T(8,128)(2,1)} %bitcast.15), calls=%async_computation.2 | async-start | bytes 1048576 | tf_op jit(solution)/shard_map/all_to_all | solution.py:92
  24.1 57.2 %collective-permute-start = (bf16[1024,256]{1,0:T(8,128)(2,1)S(1)}, bf16[1024,256]{1,0:T(8,128)(2,1)S(1)}, u32[]{:S(2)}, u32[]{:S(2)}) collective-permute-start(bf16[1024,256]{1,0:T(8,128)(2,1)S(1)} %copy-done.24), channel_id=1, source_target_pairs={{0,8},{4,12},{8,0},{12,4},{1,9},{5,13},{9,1},{13,5},{2,10},{6,14},... | collective-permute-start | bytes 1572872 | tf_op jit(solution)/shard_map/ppermute | solution.py:16
  56.2 26.4 %collective-permute-start.3 = (bf16[192,1024]{1,0:T(8,128)(2,1)S(1)}, bf16[192,1024]{1,0:T(8,128)(2,1)}, u32[]{:S(2)}, u32[]{:S(2)}) collective-permute-start(bf16[192,1024]{1,0:T(8,128)(2,1)S(1)} %bitcast.226), channel_id=1, source_target_pairs={{0,1},{1,2},{2,3},{4,5},{5,6},{6,7},{8,9},{9,10},{10,11},{12,13},{... | collective-permute-start | bytes 1179656 | tf_op jit(solution)/shard_map/ppermute | solution.py:44
  78.3 62.5 %collective-permute-start.21 = (bf16[1024,256]{1,0:T(8,128)(2,1)}, bf16[1024,256]{1,0:T(8,128)(2,1)}, u32[]{:S(2)}, u32[]{:S(2)}) collective-permute-start(bf16[1024,256]{1,0:T(8,128)(2,1)} %bitcast.17), channel_id=1, source_target_pairs={{0,1},{1,2},{2,3},{4,5},{5,6},{6,7},{8,9},{9,10},{10,11},{12,13},{... | collective-permute-start | bytes 1572872 | tf_op jit(solution)/shard_map/ppermute | solution.py:44
  81.3 31.4 %collective-permute-start.20 = (bf16[1024,256]{1,0:T(8,128)(2,1)}, bf16[1024,256]{1,0:T(8,128)(2,1)}, u32[]{:S(2)}, u32[]{:S(2)}) collective-permute-start(bf16[1024,256]{1,0:T(8,128)(2,1)} %bitcast.17), channel_id=1, source_target_pairs={{1,0},{2,1},{3,2},{5,4},{6,5},{7,6},{9,8},{10,9},{11,10},{13,12},{... | collective-permute-start | bytes 1572872 | tf_op jit(solution)/shard_map/ppermute | solution.py:43
  84.8 34.6 %collective-permute-start.1 = (bf16[1024,512]{1,0:T(8,128)(2,1)S(1)}, bf16[1024,512]{1,0:T(8,128)(2,1)S(1)}, u32[]{:S(2)}, u32[]{:S(2)}) collective-permute-start(bf16[1024,512]{1,0:T(8,128)(2,1)S(1)} %pad_maximum_fusion.7), channel_id=1, source_target_pairs={{0,4},{4,0},{8,12},{12,8},{1,5},{5,1},{9,13},{13,9},{2,6},{6,2},{1... | collective-permute-start | bytes 3145736 | tf_op jit(solution)/shard_map/ppermute | solution.py:16
  106.3 35.2 %collective-permute-start.27 = (bf16[256,1024]{0,1:T(8,128)(2,1)}, bf16[256,1024]{0,1:T(8,128)(2,1)}, u32[]{:S(2)}, u32[]{:S(2)}) collective-permute-start(bf16[256,1024]{0,1:T(8,128)(2,1)} %bitcast.20), channel_id=1, source_target_pairs={{0,1},{1,2},{2,3},{4,5},{5,6},{6,7},{8,9},{9,10},{10,11},{12,13},{... | collective-permute-start | bytes 1572872 | tf_op jit(solution)/shard_map/ppermute | solution.py:44
  112.7 29.4 %collective-permute-start.26 = (bf16[256,1024]{0,1:T(8,128)(2,1)}, bf16[256,1024]{0,1:T(8,128)(2,1)}, u32[]{:S(2)}, u32[]{:S(2)}) collective-permute-start(bf16[256,1024]{0,1:T(8,128)(2,1)} %bitcast.20), channel_id=1, source_target_pairs={{1,0},{2,1},{3,2},{5,4},{6,5},{7,6},{9,8},{10,9},{11,10},{13,12},{... | collective-permute-start | bytes 1572872 | tf_op jit(solution)/shard_map/ppermute | solution.py:43
  117.1 26.3 %collective-permute-start.24 = (bf16[1024,256]{1,0:T(8,128)(2,1)}, bf16[1024,256]{1,0:T(8,128)(2,1)}, u32[]{:S(2)}, u32[]{:S(2)}) collective-permute-start(bf16[1024,256]{1,0:T(8,128)(2,1)} %collective-permute-done.20), channel_id=1, source_target_pairs={{1,0},{2,1},{5,4},{6,5},{9,8},{10,9},{13,12},{14,13},{17,16},{18,1... | collective-permute-start | bytes 1572872 | tf_op jit(solution)/shard_map/ppermute | solution.py:43
  143.5 32.6 %collective-permute-start.25 = (bf16[1024,256]{1,0:T(8,128)(2,1)}, bf16[1024,256]{1,0:T(8,128)(2,1)S(1)}, u32[]{:S(2)}, u32[]{:S(2)}) collective-permute-start(bf16[1024,256]{1,0:T(8,128)(2,1)} %collective-permute-done.24), channel_id=1, source_target_pairs={{1,0},{5,4},{9,8},{13,12},{17,16},{21,20},{25,24},{29,28}} | collective-permute-start | bytes 1572872 | tf_op jit(solution)/shard_map/ppermute | solution.py:43
  228.7 27.4 %collective-permute-start.35 = (bf16[256,1024]{1,0:T(8,128)(2,1)}, bf16[256,1024]{1,0:T(8,128)(2,1)}, u32[]{:S(2)}, u32[]{:S(2)}) collective-permute-start(bf16[256,1024]{1,0:T(8,128)(2,1)} %get-tuple-element.68), channel_id=1, source_target_pairs={{0,4},{4,0},{8,12},{12,8},{1,5},{5,1},{9,13},{13,9},{2,6},{6,2},{1... | collective-permute-start | bytes 1572872 | tf_op jit(solution)/shard_map/ppermute | solution.py:16
  263.1 28.9 %collective-permute-start.68 = (bf16[256,1024]{0,1:T(8,128)(2,1)}, bf16[256,1024]{0,1:T(8,128)(2,1)}, u32[]{:S(2)}, u32[]{:S(2)}) collective-permute-start(bf16[256,1024]{0,1:T(8,128)(2,1)} %get-tuple-element.84), channel_id=1, source_target_pairs={{0,1},{4,5},{8,9},{12,13},{16,17},{20,21},{24,25},{28,29}} | collective-permute-start | bytes 1572872 | tf_op jit(solution)/shard_map/ppermute | solution.py:57
  292.0 30.0 %collective-permute-start.38 = (bf16[256,1024]{1,0:T(8,128)(2,1)}, bf16[256,1024]{1,0:T(8,128)(2,1)S(1)}, u32[]{:S(2)}, u32[]{:S(2)}) collective-permute-start(bf16[256,1024]{1,0:T(8,128)(2,1)} %get-tuple-element.92), channel_id=1, source_target_pairs={{0,4},{4,0},{8,12},{12,8},{1,5},{5,1},{9,13},{13,9},{2,6},{6,2},{1... | collective-permute-start | bytes 1572872 | tf_op jit(solution)/shard_map/ppermute | solution.py:16
  344.7 44.4 %collective-permute-start.74 = (bf16[256,1024]{0,1:T(8,128)(2,1)}, bf16[256,1024]{0,1:T(8,128)(2,1)}, u32[]{:S(2)}, u32[]{:S(2)}) collective-permute-start(bf16[256,1024]{0,1:T(8,128)(2,1)} %add_convert_fusion.1), channel_id=1, source_target_pairs={{0,16},{16,0},{1,17},{17,1},{2,18},{18,2},{3,19},{19,3},{4,20},{20... | collective-permute-start | bytes 1572872 | tf_op jit(solution)/shard_map/ppermute | solution.py:16
  354.8 114.9 %collective-permute-start.67 = (bf16[1024,256]{1,0:T(8,128)(2,1)}, bf16[1024,256]{1,0:T(8,128)(2,1)}, u32[]{:S(2)}, u32[]{:S(2)}) collective-permute-start(bf16[1024,256]{1,0:T(8,128)(2,1)} %add_convert_fusion.5), channel_id=1, source_target_pairs={{0,16},{16,0},{1,17},{17,1},{2,18},{18,2},{3,19},{19,3},{4,20},{20... | collective-permute-start | bytes 1572872 | tf_op jit(solution)/shard_map/ppermute | solution.py:16
  391.2 96.9 %all-to-all-start.10 = ((bf16[256,4,256]{0,2,1:T(8,128)(2,1)}), bf16[256,4,256]{0,2,1:T(8,128)(2,1)S(1)}, u32[]{:S(2)}, u32[]{:S(2)}) async-start(bf16[256,4,256]{0,2,1:T(8,128)(2,1)} %bitcast.63), calls=%async_computation.10 | async-start | bytes 1048576 | tf_op jit(solution)/shard_map/all_to_all | solution.py:92
  396.5 53.9 %collective-permute-start.54 = (bf16[64,1024]{1,0:T(8,128)(2,1)S(1)}, bf16[64,1024]{1,0:T(8,128)(2,1)S(1)}, u32[]{:S(2)}, u32[]{:S(2)}) collective-permute-start(bf16[64,1024]{1,0:T(8,128)(2,1)S(1)} %get-tuple-element.113), channel_id=1, source_target_pairs={{0,1},{4,5},{8,9},{12,13},{16,17},{20,21},{24,25},{28,29}} | collective-permute-start | bytes 393224 | tf_op jit(solution)/shard_map/ppermute | solution.py:57
  400.3 50.2 %collective-permute-start.57 = (bf16[64,1024]{1,0:T(8,128)(2,1)S(1)}, bf16[64,1024]{1,0:T(8,128)(2,1)S(1)}, u32[]{:S(2)}, u32[]{:S(2)}) collective-permute-start(bf16[64,1024]{1,0:T(8,128)(2,1)S(1)} %get-tuple-element.114), channel_id=1, source_target_pairs={{3,2},{7,6},{11,10},{15,14},{19,18},{23,22},{27,26},{31,30}} | collective-permute-start | bytes 393224 | tf_op jit(solution)/shard_map/ppermute | solution.py:58
  403.4 56.6 %collective-permute-start.47 = (bf16[192,1024]{1,0:T(8,128)(2,1)S(1)}, bf16[192,1024]{1,0:T(8,128)(2,1)S(1)}, u32[]{:S(2)}, u32[]{:S(2)}) collective-permute-start(bf16[192,1024]{1,0:T(8,128)(2,1)S(1)} %bitcast.210), channel_id=1, source_target_pairs={{0,1},{4,5},{8,9},{12,13},{16,17},{20,21},{24,25},{28,29}} | collective-permute-start | bytes 1179656 | tf_op jit(solution)/shard_map/ppermute | solution.py:57
  404.7 61.7 %collective-permute-start.50 = (bf16[192,1024]{1,0:T(8,128)(2,1)S(1)}, bf16[192,1024]{1,0:T(8,128)(2,1)}, u32[]{:S(2)}, u32[]{:S(2)}) collective-permute-start(bf16[192,1024]{1,0:T(8,128)(2,1)S(1)} %bitcast.211), channel_id=1, source_target_pairs={{3,2},{7,6},{11,10},{15,14},{19,18},{23,22},{27,26},{31,30}} | collective-permute-start | bytes 1179656 | tf_op jit(solution)/shard_map/ppermute | solution.py:58
  457.9 46.0 %collective-permute-start.45 = (bf16[1024,256]{1,0:T(8,128)(2,1)}, bf16[1024,256]{1,0:T(8,128)(2,1)}, u32[]{:S(2)}, u32[]{:S(2)}) collective-permute-start(bf16[1024,256]{1,0:T(8,128)(2,1)} %get-tuple-element.77), channel_id=1, source_target_pairs={{0,4},{4,0},{8,12},{12,8},{1,5},{5,1},{9,13},{13,9},{2,6},{6,2},{1... | collective-permute-start | bytes 1572872 | tf_op jit(solution)/shard_map/ppermute | solution.py:16
  458.5 76.8 %collective-permute-start.44 = (bf16[1024,256]{1,0:T(8,128)(2,1)}, bf16[1024,256]{1,0:T(8,128)(2,1)}, u32[]{:S(2)}, u32[]{:S(2)}) collective-permute-start(bf16[1024,256]{1,0:T(8,128)(2,1)} %get-tuple-element.76), channel_id=1, source_target_pairs={{0,4},{4,0},{8,12},{12,8},{1,5},{5,1},{9,13},{13,9},{2,6},{6,2},{1... | collective-permute-start | bytes 1572872 | tf_op jit(solution)/shard_map/ppermute | solution.py:16
  483.7 28.3 %collective-permute-start.49 = (bf16[192,1024]{1,0:T(8,128)(2,1)}, bf16[192,1024]{1,0:T(8,128)(2,1)S(1)}, u32[]{:S(2)}, u32[]{:S(2)}) collective-permute-start(bf16[192,1024]{1,0:T(8,128)(2,1)} %add_convert_fusion.12), channel_id=1, source_target_pairs={{0,1},{1,2},{2,3},{4,5},{5,6},{6,7},{8,9},{9,10},{10,11},{12,13},{... | collective-permute-start | bytes 1179656 | tf_op jit(solution)/shard_map/ppermute | solution.py:57
  506.1 29.2 %collective-permute-start.46 = (bf16[1024,256]{1,0:T(8,128)(2,1)}, bf16[1024,256]{1,0:T(8,128)(2,1)}, u32[]{:S(2)}, u32[]{:S(2)}) collective-permute-start(bf16[1024,256]{1,0:T(8,128)(2,1)} %add_convert_fusion.8), channel_id=1, source_target_pairs={{0,8},{4,12},{8,0},{12,4},{1,9},{5,13},{9,1},{13,5},{2,10},{6,14},... | collective-permute-start | bytes 1572872 | tf_op jit(solution)/shard_map/ppermute | solution.py:16
  (137 other events, 1937.9 us)

commit v2 on v1

v2 whole, which is shorter than its diff:
```python
import jax
import jax.numpy as jnp
from jax import lax
from jax.sharding import PartitionSpec as P

HEAD_DIM = 64
SEQ_LEN = 512
norm_eps = 1e-12

f32 = jnp.float32
bf16 = jnp.bfloat16

REL = (0, 2, 1, 3)


def swap(values, axis, bit):
    size = lax.axis_size(axis)
    return lax.ppermute(values, axis, [(i, i ^ bit) for i in range(size)])


def dot(left, right, left_dim, right_dim):
    return lax.dot_general(
        left, right, (((left_dim,), (right_dim,)), ((), ())), preferred_element_type=f32
    )


def after(values, earlier):
    return lax.optimization_barrier((values, earlier))[0]


def trade(values, axis):
    return lax.all_to_all(values, axis, 0, 0, tiled=True)


def to_rel(values, dim):
    r = lax.axis_index("row")
    size = values.shape[dim] // 4
    parts = [lax.dynamic_slice_in_dim(values, (r ^ j) * size, size, dim) for j in REL]
    return jnp.concatenate(parts, dim)


def from_rel(values, dim):
    r = lax.axis_index("row")
    size = values.shape[dim] // 4
    parts = []
    for a in range(4):
        j = r ^ a
        place = ((j & 1) << 1) | (j >> 1)
        parts.append(lax.dynamic_slice_in_dim(values, place * size, size, dim))
    return jnp.concatenate(parts, dim)


def row_reduce(own, across, beside, diagonal, dim):
    size = own.shape[dim]
    got = swap(jnp.concatenate([beside, diagonal], dim).astype(bf16), "row", 1)
    far = across + lax.slice_in_dim(got, size, 2 * size, axis=dim).astype(f32)
    far = swap(far.astype(bf16), "row", 2)
    return own + lax.slice_in_dim(got, 0, size, axis=dim).astype(f32) + far.astype(f32)


def line_gather(block):
    size, here = lax.axis_size("col"), lax.axis_index("col")
    up, down = [block], [block]
    for step in range(1, size):
        up.append(lax.ppermute(up[-1], "col", [(i, i - 1) for i in range(1, size - step + 1)]))
        down.append(lax.ppermute(down[-1], "col", [(i, i + 1) for i in range(step - 1, size - 1)]))
    blocks = [block] + [
        jnp.where(here + step < size, up[step], down[size - step]) for step in range(1, size)
    ]
    return blocks


def in_col_order(blocks):
    size, here = lax.axis_size("col"), lax.axis_index("col")
    out = jnp.zeros((size,) + blocks[0].shape, blocks[0].dtype)
    for step, b in enumerate(blocks):
        place = (here + step) % size
        out = lax.dynamic_update_slice_in_dim(out, b[None], place, 0)
    return out


def spread(block, axis):
    return trade(jnp.broadcast_to(block[None], (lax.axis_size(axis),) + block.shape), axis)


def normalize(resid):
    row_mean = jnp.mean(resid, 1, keepdims=True)
    centered = resid - row_mean
    variance = jnp.mean(centered * centered, 1, keepdims=True)
    inv_std = lax.rsqrt(variance + norm_eps)
    return centered * inv_std, inv_std


def norm_backward(incoming, normed, inv_std, gain):
    scaled = incoming * gain
    return inv_std * (
        scaled
        - jnp.mean(scaled, 1, keepdims=True)
        - normed * jnp.mean(scaled * normed, 1, keepdims=True)
    )


def dp_sum(values, first_bit):
    size = lax.axis_size("dp")
    bit = first_bit
    while bit < size:
        low = values.astype(bf16)
        values = low.astype(f32) + swap(low, "dp", bit).astype(f32)
        bit *= 2
    return values


def per_device(
    tokens,
    w_qkv,
    bias_qv,
    w_out,
    bias_out,
    gain_one,
    shift_one,
    w_in,
    bias_in,
    w_back,
    bias_back,
    gain_two,
    shift_two,
    cotangent,
):
    rows, cols = lax.axis_size("row"), lax.axis_size("col")
    r, n = lax.axis_index("row"), lax.axis_index("dp") & 1
    dp_size = lax.axis_size("dp")
    group, width_local = tokens.shape
    block = group // rows
    width = width_local * rows
    heads_tile = w_qkv.shape[2]
    head_piece = heads_tile // rows
    heads_width = cols * head_piece
    hid_tile = w_in.shape[1]
    hid_piece = hid_tile // rows
    half = hid_piece // 2
    hid_half = cols * half
    seq_count = group // SEQ_LEN
    head_count = heads_width // HEAD_DIM
    score_scale = HEAD_DIM ** (-0.5)
    seq_shape = (seq_count, SEQ_LEN, head_count, HEAD_DIM)

    wq = jnp.transpose(w_qkv, (2, 0, 1)).reshape(rows, head_piece, 3, width_local)
    wq = trade(jnp.transpose(wq, (0, 2, 1, 3)).reshape(rows, 3 * head_piece, width_local), "row")
    wq = to_rel(jnp.transpose(wq, (1, 0, 2)).reshape(3 * head_piece, width), 1)
    hid_bias = lax.dynamic_slice(bias_in, (r * hid_piece,), (hid_piece,))
    head_bias = lax.dynamic_slice(bias_qv, (0, r * head_piece), (2, head_piece)).reshape(-1)
    bias_row = jnp.concatenate([hid_bias, head_bias])
    bias_rows = jnp.pad(bias_row[None], ((0, 15), (0, width - bias_row.shape[0])))
    line = line_gather(jnp.concatenate([wq, bias_rows], 0))
    wq_all = in_col_order([b[: 3 * head_piece].reshape(3, head_piece, width) for b in line])
    wq_all = jnp.transpose(wq_all, (1, 0, 2, 3)).reshape(3 * heads_width, width)
    col_bias = in_col_order([b[3 * head_piece, : bias_row.shape[0]] for b in line]).astype(f32)
    bias_q = col_bias[:, hid_piece : hid_piece + head_piece].reshape(-1)
    bias_v = col_bias[:, hid_piece + head_piece :].reshape(-1)

    def own_first(values):
        parts = [
            lax.dynamic_slice_in_dim(values, k * half, half, 1).reshape(hid_half)
            for k in (n, 1 - n)
        ]
        return jnp.concatenate(parts)

    bias_in_f = own_first(col_bias[:, :hid_piece])

    across = swap(tokens, "row", 2)
    beside = swap(tokens, "row", 1)
    diagonal = swap(across, "row", 1)
    tokens_all = jnp.concatenate([tokens, across, beside, diagonal], 1)

    wi = jnp.transpose(w_in).reshape(rows, hid_piece, width_local)
    wi = lax.dynamic_slice_in_dim(wi, n * half, half, 1)
    wb = w_back.reshape(rows, hid_piece, width_local)
    wb = lax.dynamic_slice_in_dim(wb, n * half, half, 1)
    wo = w_out.reshape(rows, head_piece, width_local)
    vectors = jnp.stack([bias_out, gain_one, shift_one, bias_back, gain_two, shift_two])
    vectors = jnp.pad(vectors, ((0, 10), (0, 0)))
    vectors = jnp.broadcast_to(vectors[None], (rows,) + vectors.shape)
    mixed = trade(jnp.concatenate([wi, wb, wo, vectors], 1), "row")
    mixed = jnp.transpose(mixed, (1, 0, 2)).reshape(-1, width)
    wi, wb = mixed[:half], mixed[half : 2 * half]
    wo = mixed[2 * half : 2 * half + head_piece]
    vectors = mixed[2 * half + head_piece :].astype(f32)
    bias_out_f, gain_one_f, shift_one_f, bias_back_f, gain_two_f, shift_two_f = [
        vectors[i] for i in range(6)
    ]
    wi = lax.all_gather(wi, "col", axis=0, tiled=True)
    wo_all = spread(after(wo, line[-1]), "col").reshape(heads_width, width)
    wb = spread(after(wb, line[-1]), "col").reshape(hid_half, width)
    wi_all = jnp.concatenate([wi, swap(wi, "dp", 1)], 0)
    wb_all = jnp.concatenate([wb, swap(wb, "dp", 1)], 0)
    cot = after(cotangent, line[-1]).reshape(rows, block, width_local)
    cot = jnp.transpose(trade(cot, "row"), (1, 0, 2)).reshape(block, width).astype(f32)

    joined = dot(tokens_all, wq_all, 1, 1)
    queries = (joined[:, :heads_width] + bias_q).astype(bf16).reshape(seq_shape)
    key_rows = joined[:, heads_width : 2 * heads_width].astype(bf16).reshape(seq_shape)
    value_rows = (joined[:, 2 * heads_width :] + bias_v).astype(bf16).reshape(seq_shape)
    scores = (
        jnp.einsum("sqhd,skhd->shqk", queries, key_rows, preferred_element_type=f32) * score_scale
    )
    row_peak = jnp.max(scores, -1, keepdims=True)
    expo_scores = jnp.exp(scores - row_peak)
    row_total = jnp.sum(expo_scores, -1, keepdims=True)
    attn_weights = expo_scores / row_total
    log_total = row_peak + jnp.log(row_total)
    context = jnp.einsum(
        "shqk,skhd->sqhd", attn_weights.astype(bf16), value_rows, preferred_element_type=f32
    )
    context = to_rel(context.reshape(group, heads_width).astype(bf16), 0)

    send = dot(context[2 * block :], wo_all, 1, 0).astype(bf16)
    keep = dot(context[: 2 * block], wo_all, 1, 0)
    attended = row_reduce(keep[:block], keep[block:], send[:block], send[block:], 0) + bias_out_f
    tokens_own = lax.dynamic_slice_in_dim(tokens_all, r * block, block, 0)
    tokens_own = from_rel(tokens_own, 1).astype(f32)
    normed_one, inv_one = normalize(tokens_own + attended)
    hidden_one = normed_one * gain_one_f + shift_one_f

    def chips(values):
        over = swap(values, "row", 2)
        near = jnp.concatenate([values, swap(values, "row", 1)], 0)
        return near, jnp.concatenate([over, swap(over, "row", 1)], 0)

    def reduce_chips(near, far):
        return row_reduce(near[:block], far[:block], near[block:], far[block:], 0)

    hidden = chips(hidden_one.astype(bf16))
    pre_act, cdf, activated, mlp = [], [], [], []
    for h in hidden:
        pre = dot(h, wi_all, 1, 1) + bias_in_f
        pre_act.append(pre)
        cdf.append(0.5 * (1.0 + lax.erf(pre * 0.7071067811865476)))
        activated.append((pre * cdf[-1]).astype(bf16))
        mlp.append(dot(activated[-1], wb_all, 1, 0))
    mlp_out = reduce_chips(*mlp) + bias_back_f
    normed_two, inv_two = normalize(hidden_one + mlp_out)
    output = (normed_two * gain_two_f + shift_two_f).astype(bf16)

    d_two = norm_backward(cot, normed_two, inv_two, gain_two_f)
    d_mlp_low = d_two.astype(bf16)
    d_mlp = chips(d_mlp_low)
    d_pre, d_hid = [], []
    for k in range(2):
        d_activated = dot(d_mlp[k], wb_all, 1, 1)
        pdf = jnp.exp(-0.5 * pre_act[k] * pre_act[k]) * 0.3989422804014327
        d_pre.append((d_activated * (cdf[k] + pre_act[k] * pdf)).astype(bf16))
        d_hid.append(dot(d_pre[k], wi_all, 1, 0))
    d_hidden = d_two + reduce_chips(*d_hid)
    output = after(output, d_pre[0])
    output = lax.all_to_all(output, "row", 1, 0, tiled=True)

    def hidden_grad(left, right):
        other = sum(dot(a[:, hid_half:], b, 0, 0) for a, b in zip(left, right))
        own = sum(dot(a[:, :hid_half], b, 0, 0) for a, b in zip(left, right))
        total = own + swap(other.astype(bf16), "dp", 1).astype(f32)
        return trade(total.astype(bf16).reshape(cols, half, width), "col")

    grad_wb = hidden_grad(activated, d_mlp)
    grad_wi = hidden_grad(d_pre, hidden)
    hid_grads = jnp.stack(
        [jnp.sum(grad_wb.astype(f32), 0), jnp.sum(grad_wi.astype(f32), 0)], 0
    )
    hid_grads = dp_sum(hid_grads, 2).astype(bf16)
    others = swap(hid_grads, "dp", 1)
    hid_grads = jnp.concatenate(
        [jnp.where(n == 0, hid_grads, others), jnp.where(n == 0, others, hid_grads)], 1
    )
    hid_grads = lax.all_to_all(hid_grads, "row", 2, 1, tiled=True).astype(f32)
    grad_w_back, grad_w_in = hid_grads[0], jnp.transpose(hid_grads[1])

    d_one = norm_backward(d_hidden, normed_one, inv_one, gain_one_f)
    d_att = d_one.astype(bf16)
    over = swap(d_att, "row", 2)
    d_att_all = jnp.concatenate([d_att, over, swap(d_att, "row", 1), swap(over, "row", 1)], 0)
    d_one_cols = lax.all_to_all(after(d_one, over), "row", 1, 0, tiled=True)

    def by_owner(values):
        each = values.shape[-2]
        parts = values.reshape(cols, each, rows, width_local)
        got = trade(jnp.transpose(parts, (2, 0, 1, 3)).reshape(-1, each, width_local), ("row", "col"))
        got = jnp.sum(got.reshape(rows, cols, each, width_local).astype(f32), 1)
        return dp_sum(got, 1)

    grad_wo = dot(context, d_att_all, 0, 0).astype(bf16).reshape(cols, head_piece, width)
    grad_w_out = by_owner(grad_wo).reshape(heads_tile, width_local)

    d_context = from_rel(dot(d_att_all, wo_all, 1, 1).astype(bf16), 0).reshape(seq_shape)
    scores_again = (
        jnp.einsum("sqhd,skhd->shqk", queries, key_rows, preferred_element_type=f32) * score_scale
    )
    weights_again = jnp.exp(scores_again - log_total)
    d_value = jnp.einsum(
        "shqk,sqhd->skhd", weights_again.astype(bf16), d_context, preferred_element_type=f32
    )
    d_weights = jnp.einsum("sqhd,skhd->shqk", d_context, value_rows, preferred_element_type=f32)
    row_inner = jnp.sum(d_weights * weights_again, -1, keepdims=True)
    d_scores = (weights_again * (d_weights - row_inner)).astype(bf16)
    d_query = (
        jnp.einsum("shqk,skhd->sqhd", d_scores, key_rows, preferred_element_type=f32) * score_scale
    )
    d_key = (
        jnp.einsum("shqk,sqhd->skhd", d_scores, queries, preferred_element_type=f32) * score_scale
    )
    d_joined = jnp.concatenate(
        [
            d_query.reshape(group, heads_width),
            d_key.reshape(group, heads_width),
            d_value.reshape(group, heads_width),
        ],
        1,
    ).astype(bf16)
    grad_wq = dot(d_joined, tokens_all, 0, 0).astype(bf16)
    grad_wq = from_rel(grad_wq, 1).reshape(3, cols, head_piece, width)
    grad_wq = jnp.transpose(grad_wq, (1, 0, 2, 3)).reshape(cols, 3 * head_piece, width)
    grad_wq = by_owner(grad_wq).reshape(rows, 3, head_piece, width_local)
    grad_w_qkv = jnp.transpose(grad_wq, (1, 3, 0, 2)).reshape(3, width_local, heads_tile)

    split = 2 * width_local
    keep = dot(d_joined, wq_all[:, :split], 1, 0)
    send = dot(d_joined, wq_all[:, split:], 1, 0).astype(bf16)
    d_tokens = row_reduce(
        keep[:, :width_local],
        keep[:, width_local:],
        send[:, :width_local],
        send[:, width_local:],
        1,
    )
    grad_tokens = d_one_cols + d_tokens

    vector_grads = jnp.stack(
        [
            jnp.sum(d_att, 0, dtype=f32),
            jnp.sum(d_hidden * normed_one, 0),
            jnp.sum(d_hidden, 0),
            jnp.sum(d_mlp_low, 0, dtype=f32),
            jnp.sum(cot * normed_two, 0),
            jnp.sum(cot, 0),
        ]
    )
    vector_grads = jnp.transpose(vector_grads.reshape(6, rows, width_local), (1, 0, 2))
    hid_sums = sum(jnp.sum(d, 0, dtype=f32) for d in d_pre).reshape(2, cols, 1, half)
    hid_sums = [jnp.where(n == k, hid_sums[0], hid_sums[1]) for k in range(2)]
    hid_sums = jnp.concatenate(hid_sums, 2)
    head_sums = jnp.sum(d_joined.reshape(group, 3, cols, head_piece), 0, dtype=f32)
    head_sums = jnp.concatenate([head_sums[0], head_sums[2]], 1)
    head_sums = jnp.pad(head_sums, ((0, 0), (0, hid_piece - 2 * head_piece)))[:, None]
    col_sums = jnp.concatenate([hid_sums, head_sums], 1)
    small = jnp.concatenate(
        [
            jnp.broadcast_to(vector_grads[:, None], (rows, cols, 6, width_local)),
            jnp.broadcast_to(col_sums[None], (rows, cols, 2, width_local)),
        ],
        2,
    )
    small = jnp.broadcast_to(small[None], (dp_size,) + small.shape)
    small = trade(small.reshape(-1, 8, width_local), ("dp", "row", "col"))
    small = small.reshape(dp_size, rows, cols, 8, width_local)
    vector_grads = jnp.sum(small[:, :, :, :6], (0, 1, 2))
    col_sums = jnp.sum(small[:, :, :, 6:], (0, 2))
    grad_bias_in = col_sums[:, 0].reshape(hid_tile)
    grad_bias_qv = jnp.stack(
        [
            col_sums[:, 1, :head_piece].reshape(heads_tile),
            col_sums[:, 1, head_piece : 2 * head_piece].reshape(heads_tile),
        ]
    )

    return (
        output,
        grad_tokens,
        grad_w_qkv,
        grad_bias_qv,
        grad_w_out,
        vector_grads[0],
        vector_grads[1],
        vector_grads[2],
        grad_w_in,
        grad_bias_in,
        grad_w_back,
        vector_grads[3],
        vector_grads[4],
        vector_grads[5],
    )


def solution(mesh):
    in_specs = (
        P(("dp", "col"), "row"),
        P(None, "row", "col"),
        P(None, "col"),
        P("col", "row"),
        P("row"),
        P("row"),
        P("row"),
        P("row", "col"),
        P("col"),
        P("col", "row"),
        P("row"),
        P("row"),
        P("row"),
        P(("dp", "col"), "row"),
    )
    out_specs = (
        P(("dp", "col"), "row"),
        P(("dp", "col"), "row"),
        P(None, "row", "col"),
        P(None, "col"),
        P("col", "row"),
        P("row"),
        P("row"),
        P("row"),
        P("row", "col"),
        P("col"),
        P("col", "row"),
        P("row"),
        P("row"),
        P("row"),
    )
    return jax.shard_map(
        per_device, mesh=mesh, in_specs=in_specs, out_specs=out_specs, check_vma=False
    )
```

time: 553 us -> 529 us (0.957)
  waiting for transfers between devices: 146 us -> 237 us
  starting transfers between devices: 166 us -> 83.2 us
  blocking collectives: 59.8 us -> 0 us
  local copies, waits for them, and re-layouts: 51.3 us -> 72 us
  other arithmetic: 57.9 us -> 40.3 us
  between operations: 3.2 us -> 16 us
  matrix products: 61.9 us -> 74.6 us
    ppermute x48 -> x6, starting transfers between devices: 108 us -> 10.6 us  [the longest x3 6.8 us: line_gather(): lax.ppermute(down[-1], 'col', [(i, i + 1) for i in range(step - 1, size -...]
    ppermute x27, waiting for transfers between devices: 34.9 us -> 107 us  [swap(): return lax.ppermute(values, axis, [(i, i ^ bit) for i in range(size)])]
    ppermute x48 -> x6, waiting for transfers between devices: 75.4 us -> 23.5 us  [the longest x3 23.5 us: line_gather(): lax.ppermute(up[-1], 'col', [(i, i - 1) for i in range(1, size - step + 1)])]
    psum x1 -> x0, blocking collectives: 41.7 us -> none  [per_device(): head_sums = lax.psum(head_sums, ('dp', 'row', 'col'))]
    all_to_all x11 -> x13, waiting for transfers between devices: 35.2 us -> 73.8 us  [the longest x10 57.1 us: trade(): return lax.all_to_all(values, axis, 0, 0, tiled=True)]
    all_gather x0 -> x1, waiting for transfers between devices: none -> 32.7 us  [per_device(): wi = lax.all_gather(wi, 'col', axis=0, tiled=True)]
    all_gather x2 -> x0, blocking collectives: 18.1 us -> none  [the longest x1 12.8 us: per_device(): lax.all_gather(jnp.concatenate([hid_bias, head_bias]), 'col', axis=0)]
    convert_element_type x26 -> x9, other arithmetic: 29.4 us -> 11.5 us  [the longest x4 7.03 us: row_reduce(): far = swap(far.astype(bf16), 'row', 2)]
  transfers between devices with their start and end apart: 86 -> 47, of which waited for: 25 -> 23; matrix products, arithmetic and copies ran while one was open for 25% -> 30% of each run, Pallas kernels for 0% -> 0%
where the time goes in v2:
time: 529 us; the launch traced here: 524 us
  waiting for transfers between devices  237 us (45%)
  starting transfers between devices  83.2 us (16%)
  matrix products  74.6 us (14%)
  local copies, waits for them, and re-layouts  72 us (14%)
  other arithmetic  40.3 us (8%)
  between operations  16 us (3%)
    ppermute x27, waiting for transfers between devices, swap(): return lax.ppermute(values, axis, [(i, i ^ bit) for i in range(size)])  107 us
    all_to_all x10, waiting for transfers between devices, trade(): return lax.all_to_all(values, axis, 0, 0, tiled=True)  57.1 us
    dot_general x24, matrix products, dot(): lax.dot_general(left, right, (((left_dim,), (right_dim,)), ((), ())), pre...  57.1 us
    all_to_all x10, starting transfers between devices, trade(): return lax.all_to_all(values, axis, 0, 0, tiled=True)  41.2 us
    all_gather x1, waiting for transfers between devices, per_device(): wi = lax.all_gather(wi, 'col', axis=0, tiled=True)  32.7 us
    ppermute x3, waiting for transfers between devices, line_gather(): lax.ppermute(up[-1], 'col', [(i, i - 1) for i in range(1, size - step + 1)])  23.5 us
    unnamed x147, local copies, waits for them, and re-layouts  21.3 us
    ppermute x27, starting transfers between devices, swap(): return lax.ppermute(values, axis, [(i, i ^ bit) for i in range(size)])  17.7 us
  transfers between devices with their start and end apart: 47, of which 23 were waited for; matrix products, arithmetic and copies ran while one was open for 30% of the time, Pallas kernels for 0%

profile of v2, /device:TPU:0, one launch (start us, length us, event | category | flops | bytes accessed | tf_op | source)
XLA Modules:
  0.0 523.6 jit_solution(6807426578903891437)
XLA Ops:
  37.3 8.7 %collective-permute-done.3 = bf16[208,1024]{1,0:T(8,128)(2,1)} collective-permute-done((bf16[208,1024]{1,0:T(8,128)(2,1)}, bf16[208,1024]{1,0:T(8,128)(2,1)}, u32[]{:S(2)}, u32[]{:S(2)}) %collective-permute-start.3) | collective-permute-done | bytes 426016 | tf_op jit(solution)/shard_map/ppermute | solution.py:65
  53.1 6.6 %collective-permute-done.7 = bf16[208,1024]{1,0:T(8,128)(2,1)} collective-permute-done((bf16[208,1024]{1,0:T(8,128)(2,1)}, bf16[208,1024]{1,0:T(8,128)(2,1)}, u32[]{:S(2)}, u32[]{:S(2)}) %collective-permute-start.7) | collective-permute-done | bytes 426016 | tf_op jit(solution)/shard_map/ppermute | solution.py:65
  64.0 8.2 %collective-permute-done.8 = bf16[208,1024]{1,0:T(8,128)(2,1)S(1)} collective-permute-done((bf16[208,1024]{1,0:T(8,128)(2,1)}, bf16[208,1024]{1,0:T(8,128)(2,1)S(1)}, u32[]{:S(2)}, u32[]{:S(2)}) %collective-permute-start.8) | collective-permute-done | bytes 426016 | tf_op jit(solution)/shard_map/ppermute | solution.py:65
  111.7 5.2 all-to-all-start.3
  116.9 32.7 %all-gather.2.cloned.1.call-done = bf16[512,1024]{0,1:T(8,128)(2,1)} async-done(((bf16[128,1024]{0,1:T(8,128)(2,1)}), bf16[512,1024]{0,1:T(8,128)(2,1)}) %all-gather.2.cloned.1.call-update) | async-done | bytes 1048592 | tf_op jit(solution)/shard_map/all_gather | solution.py:191
  151.9 13.8 %collective-permute-done.14 = bf16[256,1024]{1,0:T(8,128)(2,1)S(1)} collective-permute-done((bf16[256,1024]{1,0:T(8,128)(2,1)S(1)}, bf16[256,1024]{1,0:T(8,128)(2,1)S(1)}, u32[]{:S(2)}, u32[]{:S(2)}) %collective-permute-start.14) | collective-permute-done | bytes 524320 | tf_op jit(solution)/shard_map/ppermute | solution.py:18
  166.8 8.1 %collective-permute-done.12 = bf16[512,1024]{0,1:T(8,128)(2,1)} collective-permute-done((bf16[512,1024]{0,1:T(8,128)(2,1)}, bf16[512,1024]{0,1:T(8,128)(2,1)}, u32[]{:S(2)}, u32[]{:S(2)}) %collective-permute-start.12) | collective-permute-done | bytes 1048608 | tf_op jit(solution)/shard_map/ppermute | solution.py:18
  181.6 6.1 %multiply_convert_fusion.2 = (bf16[512,1024]{1,0:T(8,128)(2,1)S(1)}, bf16[512,1024]{1,0:T(8,128)(2,1)S(1)}, f32[512,1024]{1,0:T(8,128)}) fusion(f32[1024]{0:T(1024)S(1)} %pad_maximum_fusion.22, f32[512,1024]{1,0:T(8,128)S(1)} %fusion.113, bf16[1024,1024]{0,1:T(8,128)(2,1)} %constant_dynamic-update-slice_fusion.4, ...), kind=kOutput, calls=%fused_computation.38 | convolution fusion | flops 1082130432 | bytes 9441280 | tf_op jit(solution)/shard_map/dot_general | solution.py:22
  187.7 14.0 %collective-permute-done.13 = bf16[512,1024]{1,0:T(8,128)(2,1)S(1)} collective-permute-done((bf16[512,1024]{1,0:T(8,128)(2,1)}, bf16[512,1024]{1,0:T(8,128)(2,1)S(1)}, u32[]{:S(2)}, u32[]{:S(2)}) %collective-permute-start.13) | collective-permute-done | bytes 1048608 | tf_op jit(solution)/shard_map/ppermute | solution.py:18
  217.2 5.0 all-to-all-done.4
  222.7 10.3 %collective-permute-done.17 = bf16[256,1024]{1,0:T(8,128)(2,1)S(1)} collective-permute-done((bf16[256,1024]{1,0:T(8,128)(2,1)}, bf16[256,1024]{1,0:T(8,128)(2,1)S(1)}, u32[]{:S(2)}, u32[]{:S(2)}) %collective-permute-start.17) | collective-permute-done | bytes 524320 | tf_op jit(solution)/shard_map/ppermute | solution.py:18
  237.1 13.4 %collective-permute-done.19 = bf16[256,1024]{1,0:T(8,128)(2,1)} collective-permute-done((bf16[256,1024]{1,0:T(8,128)(2,1)}, bf16[256,1024]{1,0:T(8,128)(2,1)}, u32[]{:S(2)}, u32[]{:S(2)}) %collective-permute-start.19) | collective-permute-done | bytes 524320 | tf_op jit(solution)/shard_map/ppermute | solution.py:18
  287.6 9.1 %collective-permute-done.22 = bf16[256,1024]{1,0:T(8,128)(2,1)S(1)} collective-permute-done((bf16[256,1024]{1,0:T(8,128)(2,1)S(1)}, bf16[256,1024]{1,0:T(8,128)(2,1)S(1)}, u32[]{:S(2)}, u32[]{:S(2)}) %collective-permute-start.22) | collective-permute-done | bytes 524320 | tf_op jit(solution)/shard_map/ppermute | solution.py:18
  301.2 10.7 %collective-permute-done.23 = bf16[256,1024]{1,0:T(8,128)(2,1)S(1)} collective-permute-done((bf16[256,1024]{1,0:T(8,128)(2,1)S(1)}, bf16[256,1024]{1,0:T(8,128)(2,1)S(1)}, u32[]{:S(2)}, u32[]{:S(2)}) %collective-permute-start.23) | collective-permute-done | bytes 524320 | tf_op jit(solution)/shard_map/ppermute | solution.py:18
  313.5 16.3 %collective-permute-done.30 = bf16[512,1024]{1,0:T(8,128)(2,1)S(1)} collective-permute-done((bf16[512,1024]{1,0:T(8,128)(2,1)S(1)}, bf16[512,1024]{1,0:T(8,128)(2,1)S(1)}, u32[]{:S(2)}, u32[]{:S(2)}) %collective-permute-start.30) | collective-permute-done | bytes 1048608 | tf_op jit(solution)/shard_map/ppermute | solution.py:18
  333.2 4.9 all-to-all-start.11
  349.1 14.6 %all-to-all-done.11 = bf16[4,128,1024]{2,1,0:T(8,128)(2,1)S(1)} async-done(((bf16[4,128,1024]{2,1,0:T(8,128)(2,1)}), bf16[4,128,1024]{2,1,0:T(8,128)(2,1)S(1)}, u32[]{:S(2)}, u32[]{:S(2)}) %all-to-all-start.11) | async-done | bytes 1048608 | tf_op jit(solution)/shard_map/all_to_all | solution.py:32
  367.9 5.0 fusion.29
  383.6 9.6 %all-to-all-done.10 = bf16[4,128,1024]{2,1,0:T(8,128)(2,1)} async-done(((bf16[4,128,1024]{2,1,0:T(8,128)(2,1)}), bf16[4,128,1024]{2,1,0:T(8,128)(2,1)}, u32[]{:S(2)}, u32[]{:S(2)}) %all-to-all-start.10) | async-done | bytes 1048608 | tf_op jit(solution)/shard_map/all_to_all | solution.py:32
  415.5 11.1 %collective-permute-done.32 = bf16[2,128,1024]{2,1,0:T(8,128)(2,1)S(1)} collective-permute-done((bf16[2,128,1024]{2,1,0:T(8,128)(2,1)S(1)}, bf16[2,128,1024]{2,1,0:T(8,128)(2,1)S(1)}, u32[]{:S(2)}, u32[]{:S(2)}) %collective-permute-start.32) | collective-permute-done | bytes 524320 | tf_op jit(solution)/shard_map/ppermute | solution.py:18
  441.2 6.6 %all-to-all-done.12 = bf16[2,256,1024]{1,0,2:T(2,128)(2,1)} async-done(((bf16[2,256,1024]{1,0,2:T(2,128)(2,1)}), bf16[2,256,1024]{1,0,2:T(2,128)(2,1)}, u32[]{:S(2)}, u32[]{:S(2)}) %all-to-all-start.12) | async-done | bytes 1048608 | tf_op jit(solution)/shard_map/all_to_all | solution.py:273
  447.8 4.8 all-to-all-start.7
  470.5 20.4 %all-to-all-done.7 = bf16[16,192,256]{2,1,0:T(8,128)(2,1)S(1)} async-done(((bf16[16,192,256]{2,1,0:T(8,128)(2,1)}), bf16[16,192,256]{2,1,0:T(8,128)(2,1)S(1)}, u32[]{:S(2)}, u32[]{:S(2)}) %all-to-all-start.7) | async-done | bytes 1572896 | tf_op jit(solution)/shard_map/all_to_all | solution.py:32
  499.5 10.1 %all-to-all-done.6 = f32[256,4,256]{2,0,1:T(8,128)} async-done(((f32[256,4,256]{2,0,1:T(8,128)}), f32[256,4,256]{2,0,1:T(8,128)}, u32[]{:S(2)}, u32[]{:S(2)}) %all-to-all-start.6) | async-done | bytes 1048608 | tf_op jit(solution)/shard_map/all_to_all | solution.py:280
  (413 shorter events, 252.4 us)
Async XLA Ops:
  13.5 22.0 %collective-permute-start = (bf16[1024,256]{1,0:T(8,128)(2,1)}, bf16[1024,256]{1,0:T(8,128)(2,1)}, u32[]{:S(2)}, u32[]{:S(2)}) collective-permute-start(bf16[1024,256]{1,0:T(8,128)(2,1)} %param.14), channel_id=1, source_target_pairs={{0,8},{4,12},{8,0},{12,4},{1,9},{5,13},{9,1},{13,5},{2,10},{6,14},... | collective-permute-start | bytes 1572872 | tf_op jit(solution)/shard_map/ppermute | solution.py:18
  28.2 19.2 %all-to-all-start.1 = ((bf16[4,336,256]{2,1,0:T(8,128)(2,1)}), bf16[4,336,256]{2,1,0:T(8,128)(2,1)S(1)}, u32[]{:S(2)}, u32[]{:S(2)}) async-start(bf16[4,336,256]{2,1,0:T(8,128)(2,1)} %pad_maximum_fusion.8), calls=%async_computation.1 | async-start | bytes 1376256 | tf_op jit(solution)/shard_map/all_to_all | solution.py:32
  33.0 17.3 %collective-permute-start.1 = (bf16[1024,256]{1,0:T(8,128)(2,1)}, bf16[1024,256]{1,0:T(8,128)(2,1)S(1)}, u32[]{:S(2)}, u32[]{:S(2)}) collective-permute-start(bf16[1024,256]{1,0:T(8,128)(2,1)} %param.14), channel_id=1, source_target_pairs={{0,4},{4,0},{8,12},{12,8},{1,5},{5,1},{9,13},{13,9},{2,6},{6,2},{1... | collective-permute-start | bytes 1572872 | tf_op jit(solution)/shard_map/ppermute | solution.py:18
  74.3 25.7 %all-to-all-start.2 = ((bf16[4,64,1024]{2,1,0:T(8,128)(2,1)}), bf16[4,64,1024]{2,1,0:T(8,128)(2,1)S(1)}, u32[]{:S(2)}, u32[]{:S(2)}) async-start(bf16[4,64,1024]{2,1,0:T(8,128)(2,1)} %broadcast_in_dim.24), calls=%async_computation.2 | async-start | bytes 1048576 | tf_op jit(solution)/shard_map/all_to_all | solution.py:32
  77.8 71.8 %all-gather.2.cloned.1.call-start = ((), (), s32[]{:S(2)}) async-start(), calls=%async_computation.13 | async-start | bytes 1310720 | tf_op jit(solution)/shard_map/all_gather | solution.py:191
  106.4 43.2 %collective-permute-start.10 = (bf16[256,1024]{1,0:T(8,128)(2,1)}, bf16[256,1024]{1,0:T(8,128)(2,1)}, u32[]{:S(2)}, u32[]{:S(2)}) collective-permute-start(bf16[256,1024]{1,0:T(8,128)(2,1)} %fusion.44), channel_id=1, source_target_pairs={{0,8},{4,12},{8,0},{12,4},{1,9},{5,13},{9,1},{13,5},{2,10},{6,14},... | collective-permute-start | bytes 1572872 | tf_op jit(solution)/shard_map/ppermute | solution.py:18
  111.7 65.6 %all-to-all-start.3 = ((bf16[4,128,1024]{2,1,0:T(8,128)(2,1)}), bf16[4,128,1024]{2,1,0:T(8,128)(2,1)}, u32[]{:S(2)}, u32[]{:S(2)}) async-start(bf16[4,128,1024]{2,1,0:T(8,128)(2,1)} %broadcast_in_dim.25), calls=%async_computation.3 | async-start | bytes 2097152 | tf_op jit(solution)/shard_map/all_to_all | solution.py:32
  149.5 25.4 %collective-permute-start.12 = (bf16[512,1024]{0,1:T(8,128)(2,1)}, bf16[512,1024]{0,1:T(8,128)(2,1)}, u32[]{:S(2)}, u32[]{:S(2)}) collective-permute-start(bf16[512,1024]{0,1:T(8,128)(2,1)} %all-gather.2.cloned.1.call-done), channel_id=1, source_target_pairs={{0,16},{16,0},{1,17},{17,1},{2,18},{18,2},{3,19},{19,3},{4,20},{20... | collective-permute-start | bytes 3145736 | tf_op jit(solution)/shard_map/ppermute | solution.py:18
  177.2 24.4 %collective-permute-start.13 = (bf16[512,1024]{1,0:T(8,128)(2,1)}, bf16[512,1024]{1,0:T(8,128)(2,1)S(1)}, u32[]{:S(2)}, u32[]{:S(2)}) collective-permute-start(bf16[512,1024]{1,0:T(8,128)(2,1)} %bitcast.29), channel_id=1, source_target_pairs={{0,16},{16,0},{1,17},{17,1},{2,18},{18,2},{3,19},{19,3},{4,20},{20... | collective-permute-start | bytes 3145736 | tf_op jit(solution)/shard_map/ppermute | solution.py:18
  215.3 17.7 %collective-permute-start.17 = (bf16[256,1024]{1,0:T(8,128)(2,1)}, bf16[256,1024]{1,0:T(8,128)(2,1)S(1)}, u32[]{:S(2)}, u32[]{:S(2)}) collective-permute-start(bf16[256,1024]{1,0:T(8,128)(2,1)} %fusion.40), channel_id=1, source_target_pairs={{0,8},{4,12},{8,0},{12,4},{1,9},{5,13},{9,1},{13,5},{2,10},{6,14},... | collective-permute-start | bytes 1572872 | tf_op jit(solution)/shard_map/ppermute | solution.py:18
  250.5 17.8 %collective-permute-start.20 = (bf16[256,1024]{1,0:T(8,128)(2,1)}, bf16[256,1024]{1,0:T(8,128)(2,1)}, u32[]{:S(2)}, u32[]{:S(2)}) collective-permute-start(bf16[256,1024]{1,0:T(8,128)(2,1)} %collective-permute-done.19), channel_id=1, source_target_pairs={{0,4},{4,0},{8,12},{12,8},{1,5},{5,1},{9,13},{13,9},{2,6},{6,2},{1... | collective-permute-start | bytes 1572872 | tf_op jit(solution)/shard_map/ppermute | solution.py:18
  260.6 72.6 %all-to-all-start.5 = ((bf16[256,4,256]{2,0,1:T(8,128)(2,1)}), bf16[256,4,256]{2,0,1:T(8,128)(2,1)}, u32[]{:S(2)}, u32[]{:S(2)}) async-start(bf16[256,4,256]{2,0,1:T(8,128)(2,1)} %bitcast.226), calls=%async_computation.5 | async-start | bytes 1048576 | tf_op jit(solution)/shard_map/all_to_all | solution.py:255
  281.8 30.1 %collective-permute-start.31 = (bf16[512,1024]{1,0:T(8,128)(2,1)S(1)}, bf16[512,1024]{1,0:T(8,128)(2,1)S(1)}, u32[]{:S(2)}, u32[]{:S(2)}) collective-permute-start(bf16[512,1024]{1,0:T(8,128)(2,1)S(1)} %add_convert_fusion.1), channel_id=1, source_target_pairs={{0,16},{16,0},{1,17},{17,1},{2,18},{18,2},{3,19},{19,3},{4,20},{20... | collective-permute-start | bytes 3145736 | tf_op jit(solution)/shard_map/ppermute | solution.py:18
  285.3 44.5 %collective-permute-start.30 = (bf16[512,1024]{1,0:T(8,128)(2,1)S(1)}, bf16[512,1024]{1,0:T(8,128)(2,1)S(1)}, u32[]{:S(2)}, u32[]{:S(2)}) collective-permute-start(bf16[512,1024]{1,0:T(8,128)(2,1)S(1)} %add_convert_fusion.3), channel_id=1, source_target_pairs={{0,16},{16,0},{1,17},{17,1},{2,18},{18,2},{3,19},{19,3},{4,20},{20... | collective-permute-start | bytes 3145736 | tf_op jit(solution)/shard_map/ppermute | solution.py:18
  301.1 30.4 %collective-permute-start.24 = (bf16[256,1024]{1,0:T(8,128)(2,1)S(1)}, bf16[256,1024]{1,0:T(8,128)(2,1)S(1)}, u32[]{:S(2)}, u32[]{:S(2)}) collective-permute-start(bf16[256,1024]{1,0:T(8,128)(2,1)S(1)} %get-tuple-element.108), channel_id=1, source_target_pairs={{0,4},{4,0},{8,12},{12,8},{1,5},{5,1},{9,13},{13,9},{2,6},{6,2},{1... | collective-permute-start | bytes 1572872 | tf_op jit(solution)/shard_map/ppermute | solution.py:18
  311.9 19.6 %collective-permute-start.25 = (bf16[256,1024]{1,0:T(8,128)(2,1)S(1)}, bf16[256,1024]{1,0:T(8,128)(2,1)S(1)}, u32[]{:S(2)}, u32[]{:S(2)}) collective-permute-start(bf16[256,1024]{1,0:T(8,128)(2,1)S(1)} %collective-permute-done.23), channel_id=1, source_target_pairs={{0,4},{4,0},{8,12},{12,8},{1,5},{5,1},{9,13},{13,9},{2,6},{6,2},{1... | collective-permute-start | bytes 1572872 | tf_op jit(solution)/shard_map/ppermute | solution.py:18
  333.2 30.4 %all-to-all-start.11 = ((bf16[4,128,1024]{2,1,0:T(8,128)(2,1)}), bf16[4,128,1024]{2,1,0:T(8,128)(2,1)S(1)}, u32[]{:S(2)}, u32[]{:S(2)}) async-start(bf16[4,128,1024]{2,1,0:T(8,128)(2,1)} %bitcast.72), calls=%async_computation.11 | async-start | bytes 2097152 | tf_op jit(solution)/shard_map/all_to_all | solution.py:32
  363.7 29.5 %all-to-all-start.10 = ((bf16[4,128,1024]{2,1,0:T(8,128)(2,1)}), bf16[4,128,1024]{2,1,0:T(8,128)(2,1)}, u32[]{:S(2)}, u32[]{:S(2)}) async-start(bf16[4,128,1024]{2,1,0:T(8,128)(2,1)} %bitcast.70), calls=%async_computation.10 | async-start | bytes 2097152 | tf_op jit(solution)/shard_map/all_to_all | solution.py:32
  408.5 20.3 %all-to-all-start.9 = ((bf16[16,64,256]{2,1,0:T(8,128)(2,1)}), bf16[16,64,256]{2,1,0:T(8,128)(2,1)S(1)}, u32[]{:S(2)}, u32[]{:S(2)}) async-start(bf16[16,64,256]{2,1,0:T(8,128)(2,1)} %bitcast.64), calls=%async_computation.9 | async-start | bytes 1048576 | tf_op jit(solution)/shard_map/all_to_all | solution.py:32
  428.8 18.9 %all-to-all-start.12 = ((bf16[2,256,1024]{1,0,2:T(2,128)(2,1)}), bf16[2,256,1024]{1,0,2:T(2,128)(2,1)}, u32[]{:S(2)}, u32[]{:S(2)}) async-start(bf16[2,256,1024]{1,0,2:T(2,128)(2,1)} %copy.271), calls=%async_computation.12 | async-start | bytes 2097152 | tf_op jit(solution)/shard_map/all_to_all | solution.py:273
  447.8 43.1 %all-to-all-start.7 = ((bf16[16,192,256]{2,1,0:T(8,128)(2,1)}), bf16[16,192,256]{2,1,0:T(8,128)(2,1)S(1)}, u32[]{:S(2)}, u32[]{:S(2)}) async-start(bf16[16,192,256]{2,1,0:T(8,128)(2,1)} %bitcast.46), calls=%async_computation.7 | async-start | bytes 3145728 | tf_op jit(solution)/shard_map/all_to_all | solution.py:32
  466.3 43.4 %collective-permute-start.27 = (bf16[1024,256]{1,0:T(8,128)(2,1)}, bf16[1024,256]{1,0:T(8,128)(2,1)}, u32[]{:S(2)}, u32[]{:S(2)}) collective-permute-start(bf16[1024,256]{1,0:T(8,128)(2,1)} %fusion.34), channel_id=1, source_target_pairs={{0,8},{4,12},{8,0},{12,4},{1,9},{5,13},{9,1},{13,5},{2,10},{6,14},... | collective-permute-start | bytes 1572872 | tf_op jit(solution)/shard_map/ppermute | solution.py:18
  490.8 18.8 %all-to-all-start.6 = ((f32[256,4,256]{2,0,1:T(8,128)}), f32[256,4,256]{2,0,1:T(8,128)}, u32[]{:S(2)}, u32[]{:S(2)}) async-start(f32[256,4,256]{2,0,1:T(8,128)} %bitcast.214), calls=%async_computation.6 | async-start | bytes 2097152 | tf_op jit(solution)/shard_map/all_to_all | solution.py:280
  495.5 16.9 %collective-permute-start.28 = (bf16[4,192,256]{2,1,0:T(8,128)(2,1)S(1)}, bf16[4,192,256]{2,1,0:T(8,128)(2,1)}, u32[]{:S(2)}, u32[]{:S(2)}) collective-permute-start(bf16[4,192,256]{2,1,0:T(8,128)(2,1)S(1)} %bitcast_reduce_fusion), channel_id=1, source_target_pairs={{0,16},{16,0},{1,17},{17,1},{2,18},{18,2},{3,19},{19,3},{4,20},{20... | collective-permute-start | bytes 1179656 | tf_op jit(solution)/shard_map/ppermute | solution.py:18
  (88 other events, 769.6 us)
Sparse Core Ops, SparseCore 0:
  102.4 47.0 all-gather.1
